TPU v7x, 512 devices: a whole 4x4x16 slice. The times are simulated.
512 devices in a mesh: dp: 2 (over z_hi), seq: 64 (over x, z_lo, core), tp: 4 (over y).
Axes of the slice: x: 4, y: 4, z: 16 (z_hi: 2, z_lo: 8; z = z_hi * 8 + z_lo), core: 2. Of those that a mesh axis runs over, the one named last changes fastest.
Arguments:
- tokens: bfloat16 [2, 128, 64, 1152], P('dp', 'seq', None, 'tp'), may hold values from -6 to 6
- modulation: float32 [2, 6, 1152], P('dp'), may hold values from -2 to 2, as said below
- qkv_spatial: bfloat16 [1152, 3, 1152], P('seq', None, 'tp'), may hold values from -0.1875 to 0.1875
- out_spatial: bfloat16 [1152, 1152], P('seq', 'tp'), may hold values from -0.1875 to 0.1875
- qkv_temporal: bfloat16 [1152, 3, 1152], P('seq', None, 'tp'), may hold values from -0.1875 to 0.1875
- out_temporal: bfloat16 [1152, 1152], P('seq', 'tp'), may hold values from -0.1875 to 0.1875
- cotangent: bfloat16 [2, 128, 64, 1152], P('dp', 'seq', None, 'tp'), may hold values from -6 to 6
Outputs:
- output: bfloat16 [2, 128, 64, 1152], P('dp', 'seq', None, 'tp')
- input_grad: bfloat16 [2, 128, 64, 1152], P('dp', 'seq', None, 'tp')
- out_spatial_grad: float32 [1152, 1152], P('seq', 'tp')
- out_temporal_grad: float32 [1152, 1152], P('seq', 'tp')
Inputs may be any that keep to these rules, and one draw needn't show every extreme that they name: `modulation`: rows 0, 3 are shifts, rows 1, 4 scales, rows 2, 5 gates; every gate lies in 0.5 to 1.5, every scale in -0.5 to 1.
All inputs are finite; a program needn't handle non-finite values.
Results may differ from a plain program's by a relative error of at most 0.039.
Values may be sent and summed in bfloat16 or wider, within the bound.
A program may use at most 64 MiB of HBM per device.

v0:
```python
import jax
import jax.numpy as jnp
from jax import lax
from jax.sharding import PartitionSpec as P

HD = 72


EPS = 1e-06
SPATIAL = ("gshe,gthe->ghst", "ghst,gthe->gshe", "ghst,gshe->gthe")
TEMPORAL = ("sghe,tghe->ghst", "ghst,tghe->sghe", "ghst,sghe->tghe")


def contract(form, left, right):
    return jnp.einsum(form, left, right, preferred_element_type=jnp.float32)


def norm_forward(wide, shift, scale):
    values = wide.astype(jnp.float32)
    center = values - jnp.mean(values, axis=-1, keepdims=True)
    inverse = lax.rsqrt(jnp.mean(center * center, axis=-1, keepdims=True) + EPS)
    normed = center * inverse
    return ((normed * (1.0 + scale) + shift).astype(jnp.bfloat16), normed, inverse)


def likelihood_of(query, keys, forms):
    scores = contract(forms[0], query, keys) * query.shape[-1] ** (-0.5)
    largest = jnp.max(scores, axis=-1, keepdims=True)
    weights = jnp.exp(scores - largest)
    return weights / jnp.sum(weights, axis=-1, keepdims=True)


def attend(query, keys, values, forms):
    rounded = likelihood_of(query, keys, forms).astype(jnp.bfloat16)
    return contract(forms[1], rounded, values).astype(jnp.bfloat16)


def attend_back(query, keys, values, grad_out, forms):
    likely = likelihood_of(query, keys, forms)
    grad_values = contract(forms[2], likely.astype(jnp.bfloat16), grad_out).astype(jnp.bfloat16)
    grad_likely = contract(forms[0], grad_out, values)
    spread = grad_likely - jnp.sum(likely * grad_likely, axis=-1, keepdims=True)
    grad_scores = (likely * spread * query.shape[-1] ** (-0.5)).astype(jnp.bfloat16)
    grad_query = contract(forms[1], grad_scores, keys).astype(jnp.bfloat16)
    grad_keys = contract(forms[2], grad_scores, query).astype(jnp.bfloat16)
    return (grad_query, grad_keys, grad_values)


def split_heads(flat):
    return flat.reshape(flat.shape[:-1] + (flat.shape[-1] // HD, HD))


def widen(rows):
    return lax.all_gather(rows, "tp", axis=2, tiled=True)


def local_forward(forms):

    def mixing(query, keys, values):
        return (attend(query, keys, values, forms), (query, keys, values))

    return mixing


def local_backward(forms):

    def mixing(kept, grad_out):
        return attend_back(kept[0], kept[1], kept[2], grad_out, forms)

    return mixing


def heads_forward(query, keys, values):
    pieces = (
        lax.all_to_all(query, "seq", split_axis=1, concat_axis=0, tiled=True),
        lax.all_to_all(keys, "seq", split_axis=1, concat_axis=0, tiled=True),
        lax.all_to_all(values, "seq", split_axis=1, concat_axis=0, tiled=True),
    )
    result = attend(pieces[0], pieces[1], pieces[2], TEMPORAL)
    result, query_p, keys_p, values_p = (result, pieces[0], pieces[1], pieces[2])
    back = lax.all_to_all(result, "seq", split_axis=0, concat_axis=1, tiled=True)
    return (back, (query_p, keys_p, values_p))


def heads_backward(kept, grad_out):
    grad_patch = lax.all_to_all(grad_out, "seq", split_axis=1, concat_axis=0, tiled=True)
    grad_query, grad_keys, grad_values = attend_back(
        kept[0], kept[1], kept[2], grad_patch, TEMPORAL
    )
    return (
        lax.all_to_all(grad_query, "seq", split_axis=0, concat_axis=1, tiled=True),
        lax.all_to_all(grad_keys, "seq", split_axis=0, concat_axis=1, tiled=True),
        lax.all_to_all(grad_values, "seq", split_axis=0, concat_axis=1, tiled=True),
    )


def block_forward(rows, in_weight, out_weight, shift, scale, gate_part, mixing):
    wide = widen(rows)
    modded, normed, inverse = norm_forward(wide, shift, scale)
    mixed = contract("abd,dch->abch", modded, in_weight).astype(jnp.bfloat16)
    query = split_heads(mixed[:, :, 0])
    keys = split_heads(mixed[:, :, 1])
    values = split_heads(mixed[:, :, 2])
    heads_out, kept = mixing(query, keys, values)
    flat = heads_out.reshape(heads_out.shape[:2] + (-1,))
    partial_value = contract("abi,oi->abo", flat, out_weight)
    attended = lax.psum_scatter(
        partial_value.astype(jnp.bfloat16), "tp", scatter_dimension=2, tiled=True
    ).astype(jnp.float32)
    new_rows = (rows.astype(jnp.float32) + gate_part * attended).astype(jnp.bfloat16)
    return (new_rows, (normed, inverse, flat, kept))


def block_backward(grad_new, saved, in_weight, out_weight, scale, gate_part, mixing, position):
    normed, inverse, flat, kept = saved
    narrow = grad_new.shape[-1]
    grad_gate = (gate_part * grad_new.astype(jnp.float32)).astype(jnp.bfloat16)
    grad_wide = widen(grad_gate)
    weight_grad = contract("abo,abi->oi", grad_wide, flat)
    grad_flat = contract("abo,oi->abi", grad_wide, out_weight).astype(jnp.bfloat16)
    grad_query, grad_keys, grad_values = mixing(kept, split_heads(grad_flat))
    stacked = jnp.stack(
        [
            grad_query.reshape(grad_flat.shape),
            grad_keys.reshape(grad_flat.shape),
            grad_values.reshape(grad_flat.shape),
        ],
        axis=2,
    )
    partial_value = contract("abch,dch->abd", stacked, in_weight)
    summed = lax.psum(partial_value.astype(jnp.bfloat16), "tp").astype(jnp.float32)
    scaled = summed * (1.0 + scale)
    first_mean = jnp.mean(scaled, axis=-1, keepdims=True)
    second_mean = jnp.mean(scaled * normed, axis=-1, keepdims=True)
    full_grad = inverse * (scaled - first_mean - normed * second_mean)
    grad_in = lax.dynamic_slice_in_dim(full_grad, position * narrow, narrow, 2)
    return ((grad_new.astype(jnp.float32) + grad_in).astype(jnp.bfloat16), weight_grad)


def on_device(tokens, modulation, qkv_spatial, out_spatial, qkv_temporal, out_temporal, cotangent):
    position = lax.axis_index("tp")
    rows = tokens[0]
    narrow = rows.shape[-1]
    modulators = modulation[0]
    gate_spatial = lax.dynamic_slice_in_dim(modulators[2], position * narrow, narrow, 0)
    gate_temporal = lax.dynamic_slice_in_dim(modulators[5], position * narrow, narrow, 0)
    spatial_in, spatial_out, temporal_in, temporal_out = (
        lax.all_gather(qkv_spatial, "seq", axis=0, tiled=True),
        lax.all_gather(out_spatial, "seq", axis=0, tiled=True),
        lax.all_gather(qkv_temporal, "seq", axis=0, tiled=True),
        lax.all_gather(out_temporal, "seq", axis=0, tiled=True),
    )
    first, saved_spatial = block_forward(
        rows,
        spatial_in,
        spatial_out,
        modulators[0],
        modulators[1],
        gate_spatial,
        local_forward(SPATIAL),
    )
    second, saved_temporal = block_forward(
        first, temporal_in, temporal_out, modulators[3], modulators[4], gate_temporal, heads_forward
    )
    first_grad, weight_temporal = block_backward(
        cotangent[0],
        saved_temporal,
        temporal_in,
        temporal_out,
        modulators[4],
        gate_temporal,
        heads_backward,
        position,
    )
    input_grad, weight_spatial = block_backward(
        first_grad,
        saved_spatial,
        spatial_in,
        spatial_out,
        modulators[1],
        gate_spatial,
        local_backward(SPATIAL),
        position,
    )
    total_spatial, total_temporal = lax.psum((weight_spatial, weight_temporal), ("dp", "seq"))
    height = out_spatial.shape[0]
    offset = lax.axis_index("seq") * height
    rows_spatial = lax.dynamic_slice_in_dim(total_spatial, offset, height, 0)
    rows_temporal = lax.dynamic_slice_in_dim(total_temporal, offset, height, 0)
    return (second[None], input_grad[None], rows_spatial, rows_temporal)


def solution(mesh):
    placed = (
        P("dp", "seq", None, "tp"),
        P("dp", None, None),
        P("seq", None, "tp"),
        P("seq", "tp"),
        P("seq", None, "tp"),
        P("seq", "tp"),
        P("dp", "seq", None, "tp"),
    )
    return jax.shard_map(
        on_device,
        mesh=mesh,
        in_specs=placed,
        out_specs=(
            P("dp", "seq", None, "tp"),
            P("dp", "seq", None, "tp"),
            P("seq", "tp"),
            P("seq", "tp"),
        ),
        check_vma=False,
    )
```

profile of v0, /device:TPU:1, one launch (start us, length us, event | category | flops | bytes accessed | tf_op | source)
XLA Modules:
  0.0 1153.7 jit_solution(11294792965042855836)
XLA Ops:
  9.0 11.4 all-gather
  21.0 135.3 %all-gather.1 = bf16[64,18,288]{2,1,0:T(8,128)(2,1)S(1)} all-gather(bf16[1,18,288]{2,1,0:T(8,128)(2,1)} %bitcast.219), channel_id=1, replica_groups=mesh['dp'=2,'seq'=64,'tp'=4] {'seq'}, dimensions={0}, use_global_device_ids=true | all-gather | bytes 673920 | tf_op jit(solution)/shard_map/all_gather | solution.py:149
  157.3 2.7 fusion.28
  166.4 19.6 %reduce-scatter.7.cloned.1.call-done = bf16[288,128]{1,0:T(8,128)(2,1)} async-done(((bf16[1152,128]{1,0:T(8,128)(2,1)}), bf16[288,128]{1,0:T(8,128)(2,1)}) %reduce-scatter.7.cloned.1.call-update) | async-done | bytes 73744
  188.0 10.0 all_gather.27
  199.0 113.7 %all-gather.8.cloned.1.call-done = bf16[1152,3,288]{2,1,0:T(4,128)(2,1)} async-done(((bf16[18,3,288]{2,1,0:T(4,128)(2,1)}), bf16[1152,3,288]{2,1,0:T(4,128)(2,1)}) %all-gather.8.cloned.1.call-update) | async-done | bytes 1990672 | tf_op jit(solution)/shard_map/all_gather | solution.py:150
  312.7 2.7 fusion.31
  316.3 7.4 all-to-all-start.2
  324.7 13.7 %all-to-all-done.2 = bf16[2,64,4,72]{3,0,2,1:T(2,128)(2,1)S(1)} async-done(((bf16[2,64,4,72]{3,0,2,1:T(2,128)(2,1)}), bf16[2,64,4,72]{3,0,2,1:T(2,128)(2,1)S(1)}, u32[]{:S(2)}, u32[]{:S(2)}) %all-to-all-start.2) | async-done | bytes 73760 | tf_op jit(solution)/shard_map/all_to_all | solution.py:76
  338.3 6.1 all-to-all-start.1
  345.3 13.7 %all-to-all-done.1 = bf16[2,64,4,72]{3,0,2,1:T(2,128)(2,1)S(1)} async-done(((bf16[2,64,4,72]{3,0,2,1:T(2,128)(2,1)}), bf16[2,64,4,72]{3,0,2,1:T(2,128)(2,1)S(1)}, u32[]{:S(2)}, u32[]{:S(2)}) %all-to-all-start.1) | async-done | bytes 73760 | tf_op jit(solution)/shard_map/all_to_all | solution.py:75
  359.0 6.1 all-to-all-start
  365.3 14.3 %all-to-all-done = bf16[2,64,4,72]{3,0,2,1:T(2,128)(2,1)S(1)} async-done(((bf16[2,64,4,72]{3,0,2,1:T(2,128)(2,1)}), bf16[2,64,4,72]{3,0,2,1:T(2,128)(2,1)S(1)}, u32[]{:S(2)}, u32[]{:S(2)}) %all-to-all-start) | async-done | bytes 73760 | tf_op jit(solution)/shard_map/all_to_all | solution.py:77
  381.0 6.2 all-to-all-start.3
  387.4 128.0 %all-gather.2 = bf16[64,18,288]{2,1,0:T(8,128)(2,1)S(1)} all-gather(bf16[1,18,288]{2,1,0:T(8,128)(2,1)S(1)} %bitcast.220), channel_id=1, replica_groups=mesh['dp'=2,'seq'=64,'tp'=4] {'seq'}, dimensions={0}, use_global_device_ids=true | all-gather | bytes 673920 | tf_op jit(solution)/shard_map/all_gather | solution.py:151
  519.4 20.3 %reduce-scatter.9.cloned.1.call-done = bf16[288,128]{1,0:T(8,128)(2,1)} async-done(((bf16[1152,128]{1,0:T(8,128)(2,1)}), bf16[288,128]{1,0:T(8,128)(2,1)}) %reduce-scatter.9.cloned.1.call-update) | async-done | bytes 73744
  542.3 10.4 all_gather.30
  554.0 32.7 %all_to_all.120 = bf16[2,64,4,72]{3,0,2,1:T(2,128)(2,1)S(1)} all-to-all(bf16[2,64,4,72]{3,0,2,1:T(2,128)(2,1)S(1)} %copy.113), channel_id=1, replica_groups=mesh['dp'=2,'seq'=64,'tp'=4] {'seq'}, dimensions={1} | all-to-all | bytes 147456 | tf_op jit(solution)/shard_map/all_to_all | solution.py:86
  590.0 6.1 all-to-all-start.6
  597.2 13.5 %all-to-all-done.6 = bf16[128,1,4,72]{3,2,1,0:T(4,128)(2,1)S(1)} async-done(((bf16[128,1,4,72]{3,2,1,0:T(4,128)(2,1)}), bf16[128,1,4,72]{3,2,1,0:T(4,128)(2,1)S(1)}, u32[]{:S(2)}, u32[]{:S(2)}) %all-to-all-start.6) | async-done | bytes 73760 | tf_op jit(solution)/shard_map/all_to_all | solution.py:92
  610.7 6.1 all-to-all-start.5
  617.8 13.5 %all-to-all-done.5 = bf16[128,1,4,72]{3,2,1,0:T(4,128)(2,1)S(1)} async-done(((bf16[128,1,4,72]{3,2,1,0:T(4,128)(2,1)}), bf16[128,1,4,72]{3,2,1,0:T(4,128)(2,1)S(1)}, u32[]{:S(2)}, u32[]{:S(2)}) %all-to-all-start.5) | async-done | bytes 73760 | tf_op jit(solution)/shard_map/all_to_all | solution.py:91
  631.3 6.1 all-to-all-start.7
  638.0 14.0 %all-to-all-done.7 = bf16[128,1,4,72]{3,2,1,0:T(4,128)(2,1)S(1)} async-done(((bf16[128,1,4,72]{3,2,1,0:T(4,128)(2,1)}), bf16[128,1,4,72]{3,2,1,0:T(4,128)(2,1)S(1)}, u32[]{:S(2)}, u32[]{:S(2)}) %all-to-all-start.7) | async-done | bytes 73760 | tf_op jit(solution)/shard_map/all_to_all | solution.py:93
  652.3 3.7 fusion.18
  656.0 45.5 %all-reduce.5.cloned.1.call-done = bf16[2,64,1152]{2,1,0:T(8,128)(2,1)} async-done(((bf16[2,64,1152]{2,1,0:T(8,128)(2,1)}), bf16[2,64,1152]{2,1,0:T(8,128)(2,1)}) %all-reduce.5.cloned.1.call-update) | async-done | bytes 294928 | tf_op jit(solution)/shard_map/psum | solution.py:131
  703.1 10.6 all_gather.31
  719.7 3.7 fusion.21
  723.4 1.6 convolution_bitcast_fusion
  725.1 1.7 convolution_bitcast_fusion.1
  726.8 56.6 %all-reduce.7.cloned.1.call-done = bf16[2,64,1152]{2,1,0:T(8,128)(2,1)} async-done(((bf16[2,64,1152]{2,1,0:T(8,128)(2,1)}), bf16[2,64,1152]{2,1,0:T(8,128)(2,1)}) %all-reduce.7.cloned.1.call-update) | async-done | bytes 294928 | tf_op jit(solution)/shard_map/psum | solution.py:131
  785.5 358.5 %all-reduce.9.cloned.1.call-done = (f32[1152,288]{1,0:T(8,128)}, f32[1152,288]{1,0:T(8,128)}) async-done(((f32[1152,288]{1,0:T(8,128)}, f32[1152,288]{1,0:T(8,128)}), (f32[1152,288]{1,0:T(8,128)}, f32[1152,288]{1,0:T(8,128)})) %all-reduce.9.cloned.1.call-update) | async-done | bytes 2654224 | tf_op jit(solution)/shard_map/psum | solution.py:185
  (180 shorter events, 43.4 us)
Async XLA Ops:
  7.2 150.1 %all-gather.6.cloned.1.call-start = ((), (), s32[]{:S(2)}) async-start(), calls=%async_computation.10 | async-start | bytes 3594240 | tf_op jit(solution)/shard_map/all_gather | solution.py:148
  7.9 178.0 %reduce-scatter.7.cloned.1.call-start = ((), (), s32[]{:S(2)}) async-start(), calls=%async_computation.14 | async-start | bytes 368640
  9.0 148.2 %copy-start.15 = (f32[1,6,1152]{2,0,1:T(1,128)S(1)}, f32[1,6,1152]{2,0,1:T(1,128)}, u32[]{:S(2)}) copy-start(f32[1,6,1152]{2,0,1:T(1,128)} %param.8) | copy-start | bytes 82948
  161.4 25.7 %copy-start.7 = (bf16[1,2,64,288]{3,2,1,0:T(8,128)(2,1)S(1)}, bf16[1,2,64,288]{3,2,1,0:T(8,128)(2,1)}, u32[]{:S(2)}) copy-start(bf16[1,2,64,288]{3,2,1,0:T(8,128)(2,1)} %param.7) | copy-start | bytes 221188
  165.0 147.7 %all-gather.8.cloned.1.call-start = ((), (), s32[]{:S(2)}) async-start(), calls=%async_computation.11 | async-start | bytes 3594240 | tf_op jit(solution)/shard_map/all_gather | solution.py:150
  198.7 116.6 %copy-start.25 = (f32[2,64]{1,0:T(2,128)}, f32[2,64]{1,0:T(2,128)S(1)}, u32[]{:S(2)}) copy-start(f32[2,64]{1,0:T(2,128)S(1)} %broadcast_multiply_fusion.4) | copy-start | bytes 1540
  199.0 116.6 %copy-start.23 = (f32[2,64]{1,0:T(2,128)}, f32[2,64]{1,0:T(2,128)S(1)}, u32[]{:S(2)}) copy-start(f32[2,64]{1,0:T(2,128)S(1)} %add_rsqrt_fusion) | copy-start | bytes 1540
  315.4 72.0 %copy-start.18 = (bf16[18,288]{1,0:T(8,128)(2,1)S(1)}, bf16[18,288]{1,0:T(8,128)(2,1)}, u32[]{:S(2)}) copy-start(bf16[18,288]{1,0:T(8,128)(2,1)} %param.12) | copy-start | bytes 31108
  316.3 22.0 %all-to-all-start.2 = ((bf16[2,64,4,72]{3,0,2,1:T(2,128)(2,1)}), bf16[2,64,4,72]{3,0,2,1:T(2,128)(2,1)S(1)}, u32[]{:S(2)}, u32[]{:S(2)}) async-start(bf16[2,64,4,72]{3,0,2,1:T(2,128)(2,1)} %copy.100), calls=%async_computation.2 | async-start | bytes 262144 | tf_op jit(solution)/shard_map/all_to_all | solution.py:76
  338.3 20.6 %all-to-all-start.1 = ((bf16[2,64,4,72]{3,0,2,1:T(2,128)(2,1)}), bf16[2,64,4,72]{3,0,2,1:T(2,128)(2,1)S(1)}, u32[]{:S(2)}, u32[]{:S(2)}) async-start(bf16[2,64,4,72]{3,0,2,1:T(2,128)(2,1)} %copy.98), calls=%async_computation.1 | async-start | bytes 262144 | tf_op jit(solution)/shard_map/all_to_all | solution.py:75
  359.0 20.6 %all-to-all-start = ((bf16[2,64,4,72]{3,0,2,1:T(2,128)(2,1)}), bf16[2,64,4,72]{3,0,2,1:T(2,128)(2,1)S(1)}, u32[]{:S(2)}, u32[]{:S(2)}) async-start(bf16[2,64,4,72]{3,0,2,1:T(2,128)(2,1)} %copy.96), calls=%async_computation | async-start | bytes 262144 | tf_op jit(solution)/shard_map/all_to_all | solution.py:77
  365.1 22.2 %copy-start.12 = (bf16[64,2,1,4,72]{4,1,0,3,2:T(2,128)(2,1)}, bf16[64,2,1,4,72]{4,1,0,3,2:T(2,128)(2,1)S(1)}, u32[]{:S(2)}) copy-start(bf16[64,2,1,4,72]{4,1,0,3,2:T(2,128)(2,1)S(1)} %copy.101) | copy-start | bytes 221188
  365.2 22.1 %copy-start.14 = (bf16[64,2,1,4,72]{4,1,0,3,2:T(2,128)(2,1)}, bf16[64,2,1,4,72]{4,1,0,3,2:T(2,128)(2,1)S(1)}, u32[]{:S(2)}) copy-start(bf16[64,2,1,4,72]{4,1,0,3,2:T(2,128)(2,1)S(1)} %copy.99) | copy-start | bytes 221188
  381.0 134.9 %all-to-all-start.3 = ((bf16[128,1,4,72]{3,2,1,0:T(4,128)(2,1)}), bf16[128,1,4,72]{3,2,1,0:T(4,128)(2,1)}, u32[]{:S(2)}, u32[]{:S(2)}) async-start(bf16[128,1,4,72]{3,2,1,0:T(4,128)(2,1)} %copy.106), calls=%async_computation.3 | async-start | bytes 262144 | tf_op jit(solution)/shard_map/all_to_all | solution.py:81
  387.3 152.3 %reduce-scatter.9.cloned.1.call-start = ((), (), s32[]{:S(2)}) async-start(), calls=%async_computation.15 | async-start | bytes 368640
  515.9 24.9 %copy-start.3 = (bf16[2,64,288]{2,1,0:T(8,128)(2,1)S(1)}, bf16[2,64,288]{2,1,0:T(8,128)(2,1)}, u32[]{:S(2)}) copy-start(bf16[2,64,288]{2,1,0:T(8,128)(2,1)} %copy-done.2) | copy-start | bytes 221188
  515.9 24.9 %copy-start.8 = (bf16[1,2,64,288]{3,2,1,0:T(8,128)(2,1)S(1)}, bf16[1,2,64,288]{3,2,1,0:T(8,128)(2,1)}, u32[]{:S(2)}) copy-start(bf16[1,2,64,288]{3,2,1,0:T(8,128)(2,1)} %param.13) | copy-start | bytes 221188
  552.7 43.4 %copy-start.30 = (f32[4,128]{1,0:T(4,128)S(1)}, f32[4,128]{1,0:T(4,128)}, u32[]{:S(2)}) copy-start(f32[4,128]{1,0:T(4,128)} %copy-done.29) | copy-start | bytes 6148
  553.4 42.8 %copy-start.13 = (bf16[64,2,1,4,72]{4,1,0,3,2:T(2,128)(2,1)S(1)}, bf16[64,2,1,4,72]{4,1,0,3,2:T(2,128)(2,1)}, u32[]{:S(2)}) copy-start(bf16[64,2,1,4,72]{4,1,0,3,2:T(2,128)(2,1)} %copy-done.12) | copy-start | bytes 221188
  553.7 42.4 %copy-start.28 = (f32[4,128,128]{1,2,0:T(8,128)S(1)}, f32[4,128,128]{1,2,0:T(8,128)}, u32[]{:S(2)}) copy-start(f32[4,128,128]{1,2,0:T(8,128)} %copy-done.27) | copy-start | bytes 786436
  590.0 20.6 %all-to-all-start.6 = ((bf16[128,1,4,72]{3,2,1,0:T(4,128)(2,1)}), bf16[128,1,4,72]{3,2,1,0:T(4,128)(2,1)S(1)}, u32[]{:S(2)}, u32[]{:S(2)}) async-start(bf16[128,1,4,72]{3,2,1,0:T(4,128)(2,1)} %copy.124), calls=%async_computation.6 | async-start | bytes 262144 | tf_op jit(solution)/shard_map/all_to_all | solution.py:92
  610.7 20.6 %all-to-all-start.5 = ((bf16[128,1,4,72]{3,2,1,0:T(4,128)(2,1)}), bf16[128,1,4,72]{3,2,1,0:T(4,128)(2,1)S(1)}, u32[]{:S(2)}, u32[]{:S(2)}) async-start(bf16[128,1,4,72]{3,2,1,0:T(4,128)(2,1)} %copy.119), calls=%async_computation.5 | async-start | bytes 262144 | tf_op jit(solution)/shard_map/all_to_all | solution.py:91
  631.3 20.6 %all-to-all-start.7 = ((bf16[128,1,4,72]{3,2,1,0:T(4,128)(2,1)}), bf16[128,1,4,72]{3,2,1,0:T(4,128)(2,1)S(1)}, u32[]{:S(2)}, u32[]{:S(2)}) async-start(bf16[128,1,4,72]{3,2,1,0:T(4,128)(2,1)} %copy.129), calls=%async_computation.7 | async-start | bytes 262144 | tf_op jit(solution)/shard_map/all_to_all | solution.py:93
  637.4 64.1 %all-reduce.5.cloned.1.call-start = ((), (), s32[]{:S(2)}) async-start(), calls=%async_computation.12 | async-start | bytes 589824 | tf_op jit(solution)/shard_map/psum | solution.py:131
  652.0 49.5 %copy-start.24 = (f32[2,64]{1,0:T(2,128)S(1)}, f32[2,64]{1,0:T(2,128)}, u32[]{:S(2)}) copy-start(f32[2,64]{1,0:T(2,128)} %copy-done.23) | copy-start | bytes 1540
  652.0 49.5 %copy-start.26 = (f32[2,64]{1,0:T(2,128)S(1)}, f32[2,64]{1,0:T(2,128)}, u32[]{:S(2)}) copy-start(f32[2,64]{1,0:T(2,128)} %copy-done.25) | copy-start | bytes 1540
  652.3 50.5 %copy-start.17 = (f32[288]{0:T(512)S(1)}, f32[288]{0:T(512)}, u32[]{:S(2)}) copy-start(f32[288]{0:T(512)} %copy-done.16) | copy-start | bytes 3460
  656.0 58.9 %copy-start.5 = (bf16[2,64,4,72]{3,2,1,0:T(4,128)(2,1)S(1)}, bf16[2,64,4,72]{3,2,1,0:T(4,128)(2,1)}, u32[]{:S(2)}) copy-start(bf16[2,64,4,72]{3,2,1,0:T(4,128)(2,1)} %copy-done.4) | copy-start | bytes 221188
  656.0 127.5 %all-reduce.7.cloned.1.call-start = ((), (), s32[]{:S(2)}) async-start(), calls=%async_computation.13 | async-start | bytes 589824 | tf_op jit(solution)/shard_map/psum | solution.py:131
  723.4 420.6 %all-reduce.9.cloned.1.call-start = ((), (), s32[]{:S(2)}) async-start(), calls=%async_computation.16 | async-start | bytes 7077888 | tf_op jit(solution)/shard_map/psum | solution.py:185
  725.1 58.4 %copy-start.20 = (f32[2,64]{1,0:T(2,128)S(1)}, f32[2,64]{1,0:T(2,128)}, u32[]{:S(2)}) copy-start(f32[2,64]{1,0:T(2,128)} %copy-done.19) | copy-start | bytes 1540
  725.1 58.4 %copy-start.22 = (f32[2,64]{1,0:T(2,128)S(1)}, f32[2,64]{1,0:T(2,128)}, u32[]{:S(2)}) copy-start(f32[2,64]{1,0:T(2,128)} %copy-done.21) | copy-start | bytes 1540
  (15 other events, 85.8 us)
Sparse Core Ops, SparseCore 0:
  10.2 128.6 all-gather.5
  165.1 20.8 reduce-scatter.6
  188.1 124.5 all-gather.7
  519.5 20.1 reduce-scatter.8
  656.1 45.3 all-reduce.4
  723.5 59.8 all-reduce.6
  786.9 356.9 all-reduce.8
where the time goes:
time: 1160 us; the launch traced here: 1150 us
  waiting for transfers between devices  698 us (60%)
  blocking collectives  338 us (29%)
  starting transfers between devices  44.3 us (4%)
  matrix products  26.3 us (2%)
  local copies, waits for them, and re-layouts  25.6 us (2%)
  between operations  15.1 us (1%)
    psum x1, waiting for transfers between devices, on_device(): lax.psum((weight_spatial, weight_temporal), ('dp', 'seq'))  358 us
    all_gather x1, blocking collectives, on_device(): lax.all_gather(out_spatial, 'seq', axis=0, tiled=True)  135 us
    all_gather x1, blocking collectives, on_device(): lax.all_gather(out_temporal, 'seq', axis=0, tiled=True)  128 us
    all_gather x1, waiting for transfers between devices, on_device(): lax.all_gather(qkv_temporal, 'seq', axis=0, tiled=True)  114 us
    psum x2, waiting for transfers between devices, block_backward(): lax.psum(partial_value.astype(jnp.bfloat16), 'tp').astype(jnp.float32)  102 us
    all_gather x4, blocking collectives, widen(): return lax.all_gather(rows, 'tp', axis=2, tiled=True)  42.4 us
    unnamed x9, waiting for transfers between devices  41.3 us
    all_to_all x1, blocking collectives, heads_backward(): lax.all_to_all(grad_out, 'seq', split_axis=1, concat_axis=0, tiled=True)  32.7 us
  transfers between devices with their start and end apart: 14, of which 12 were waited for; matrix products, arithmetic and copies ran while one was open for 1% of the time, Pallas kernels for 0%

commit v1 on v0

v1 whole, which is shorter than its diff:
```python
import functools

import jax
import jax.numpy as jnp
from jax import lax
from jax.experimental import pallas as pl
from jax.experimental.pallas import tpu as pltpu
from jax.sharding import PartitionSpec as P

HD = 72
EPS = 1e-06
MAIN = 16
MESH = pl.DeviceIdType.MESH
BF = jnp.bfloat16
F32 = jnp.float32


def mm(a, b):
    return lax.dot_general(a, b, (((1,), (0,)), ((), ())), preferred_element_type=F32)


def mm_nt(a, b):
    return lax.dot_general(a, b, (((1,), (1,)), ((), ())), preferred_element_type=F32)


def mm_tn(a, b):
    return lax.dot_general(a, b, (((0,), (0,)), ((), ())), preferred_element_type=F32)


def iota(shape, axis):
    return lax.broadcasted_iota(jnp.int32, shape, axis)


class Sems:
    def __init__(self):
        self.count = 0

    def take(self, n):
        first = self.count
        self.count += n
        return first


def layout(X, C, Z, Y, DP):
    s = Sems()
    names = {}
    G = X * C
    for name in ("tok", "ggt", "rs1", "fst", "rsg", "rsp", "ggs", "rsf"):
        names[name] = s.take(Y)
    for name in ("cot_x", "fst_x", "fg_x", "out_x"):
        names[name] = s.take(G)
    for name in ("cot_z", "fst_z", "fg_z", "out_z"):
        names[name] = s.take(Z)
    for name in ("zu0", "zd0", "zu0r", "zd0r", "zu1", "zd1"):
        names[name] = s.take(Z)
    names["xp0"] = s.take(15)
    names["xp1"] = s.take(X)
    names["sib0"] = s.take(2 * X)
    names["sib1"] = s.take(X)
    for b in (0, 1):
        names["wc%d" % b] = s.take(1)
        names["wx%d" % b] = s.take(X)
        names["wz%d" % b] = s.take(DP * Z)
    return names, s.count


def kernel(dims, names, tok, cot, mod, wmain, wrest, out, igrad, wg_s, wg_t, *refs):
    X, C, Z, Y, DP, T, F, H, R2 = dims
    G = X * C
    N = Y * F
    (
        ssem, rsem, pm, pr, xw_s, xw_t, gw_t, gw_s, Wm, Rb, Wr,
        cot_a, cot_b, cot_c, fst_a, fst_b, fst_c, fst_d, fg_a, fg_b, fg_c, fg_d, fg_e,
        out_a, out_b, out_c, out_d,
        mp, mpr, qkv, prob, flat_s, stat,
        rs1_a, rs1_b, rsg_a, rsg_b, rsp_a, rsp_b, rsf_a, rsf_b,
        wgp, wgc, wgx, wgxr, wgz, wgzr,
    ) = refs

    d = lax.axis_index("dp")
    s = lax.axis_index("seq")
    y = lax.axis_index("tp")
    x = s // (Z * C)
    z = lax.rem(s // C, Z)
    c = lax.rem(s, C)
    g = x * C + c
    zg = d * Z + z

    def seq_of(x_, z_, c_):
        return (x_ * Z + z_) * C + c_

    def dev(d_, x_, z_, c_, y_):
        return {"dp": d_, "seq": seq_of(x_, z_, c_), "tp": y_}

    def dev_y(y_):
        return dev(d, x, z, c, y_)

    def dev_g(g_):
        return dev(d, g_ // C, z, lax.rem(g_, C), y)

    def dev_z(z_):
        return dev(d, x, z_, c, y)

    def dev_zg(zg_):
        return dev(zg_ // Z, x, lax.rem(zg_, Z), c, y)

    def dev_x(x_):
        return dev(d, x_, z, c, y)

    sibling = dev(d, x, z, 1 - c, y)
    ZG = DP * Z
    sent = []

    def send(src, dst, sem, device):
        copy = pltpu.make_async_remote_copy(
            src_ref=src, dst_ref=dst, send_sem=ssem.at[sem], recv_sem=rsem.at[sem],
            device_id=device, device_id_type=MESH,
        )
        copy.start()
        sent.append(copy)

    def recv(dst, sem):
        pltpu.make_async_remote_copy(
            src_ref=dst, dst_ref=dst, send_sem=ssem.at[sem], recv_sem=rsem.at[sem],
            device_id=sibling, device_id_type=MESH,
        ).wait_recv()

    def ex_send(src, dst, sem, n, me, device):
        for k in range(1, n):
            peer = lax.rem(me + k, n)
            send(src(peer), dst.at[me], sem + k, device(peer))

    def ex_wait(dst, sem, n, me):
        for k in range(1, n):
            recv(dst.at[lax.rem(me + n - k, n)], sem + k)

    barrier = pltpu.get_barrier_semaphore()
    peers = [dev_y(lax.rem(y + k, Y)) for k in range(1, Y)]
    peers += [dev_g(lax.rem(g + k, G)) for k in range(1, G)]
    peers += [dev_zg(lax.rem(zg + k, ZG)) for k in range(1, ZG)]
    for peer in peers:
        pl.semaphore_signal(barrier, inc=1, device_id=peer, device_id_type=MESH)
    pl.semaphore_wait(barrier, len(peers))

    ex_send(lambda p: tok, xw_s, names["tok"], Y, y, dev_y)

    up, down = dev_zg(lax.rem(zg + 1, ZG)), dev_zg(lax.rem(zg + ZG - 1, ZG))
    nup = Z // 2
    ndown = Z - 1 - nup

    def w_slot(b, x_, c_, z_):
        return Wm.at[b, :, x_, c_, z_]

    def z_hop(step, first, b, device, sem, semr):
        z_ = lax.rem(z + first * step + Z * Z, Z)
        src = wmain.at[b] if step == 0 else w_slot(b, x, c, z_)
        send(src, w_slot(b, x, c, z_), sem + step, device)
        if b == 0:
            src = wrest if step == 0 else Rb.at[x, c, z_]
            send(src, Rb.at[x, c, z_], semr + step, device)

    def z_take(step, first, b, sem, semr):
        z_ = lax.rem(z + first * (step + 1) + Z * Z, Z)
        recv(w_slot(b, x, c, z_), sem + step)
        if b == 0:
            recv(Rb.at[x, c, z_], semr + step)

    def z_start(b):
        if nup:
            z_hop(0, -1, b, up, names["zu%d" % b], names["zu0r"])
        if ndown:
            z_hop(0, 1, b, down, names["zd%d" % b], names["zd0r"])

    def z_chain(b):
        for step in range(nup):
            z_take(step, -1, b, names["zu%d" % b], names["zu0r"])
            if step + 1 < nup:
                z_hop(step + 1, -1, b, up, names["zu%d" % b], names["zu0r"])
            if step < ndown:
                z_take(step, 1, b, names["zd%d" % b], names["zd0r"])
                if step + 1 < ndown:
                    z_hop(step + 1, 1, b, down, names["zd%d" % b], names["zd0r"])

    z_start(0)

    row = iota((T, T), 0)
    col = iota((T, T), 1)

    def swap_rows(value, source):
        return mm((col == source).astype(BF), value).astype(BF)

    def to_groups(value):
        return swap_rows(value, lax.rem(row // Z, 2) * (G * Z) + row // (2 * Z) * Z + lax.rem(row, Z))

    def from_groups(value):
        return swap_rows(
            value, lax.rem(row // Z, G) * (2 * Z) + row // (G * Z) * Z + lax.rem(row, Z)
        )

    def to_z(value):
        return swap_rows(value, lax.rem(row, 2 * G) * Z + row // (2 * G))

    def from_z(value):
        return swap_rows(value, lax.rem(row, Z) * (2 * G) + row // Z)

    def x_put(buf, value):
        buf[...] = value.reshape(G, 2 * Z, F)

    def z_put(buf, value):
        buf[...] = value.reshape(Z, 2 * G, F)

    def flatten(buf):
        return buf[...].reshape(T, F)

    x_put(cot_a, to_groups(cot[...]))
    ex_send(lambda p: cot_a.at[p], cot_b, names["cot_x"], G, g, dev_g)
    z_start(1)
    cot_b[g] = cot_a[g]
    xw_s[y] = tok[...]
    for b in (0, 1):
        for k in range(4):
            Wm[b, k, x, c, z] = wmain[b, k]
    Rb[x, c, z] = wrest[...]

    FP = pm.shape[0]
    CZ = C * Z
    j = iota((FP, CZ * MAIN), 1)
    target = (lax.rem(j // MAIN, Z) * C + j // (Z * MAIN)) * (MAIN + R2) + lax.rem(j, MAIN)
    pm[...] = (iota((FP, CZ * MAIN), 0) == target).astype(BF)
    j = iota((FP, X * CZ * R2), 1)
    target = (lax.rem(j // R2, Z) * C + lax.rem(j // (Z * R2), C)) * (MAIN + R2)
    target += MAIN + lax.rem(j, R2)
    hit = iota((FP, X * CZ * R2), 0) == target
    for x_ in range(X):
        pr[x_] = (hit & (j // (CZ * R2) == x_)).astype(BF)

    lane = iota((1, F), 1)
    head = [(lane >= h * HD) & (lane < (h + 1) * HD) for h in range(H)]

    def narrow(slices):
        rest = None
        for x_ in range(X):
            part = slices[x_]
            mp[:, x_ * CZ * MAIN : (x_ + 1) * CZ * MAIN] = mm(part, pm[:F]).astype(BF)
            more = mm(part, pr[x_, :F])
            rest = more if rest is None else rest + more
        mpr[...] = rest.astype(BF)

    def natural(main, rest, x_):
        return mm_nt(main[:, x_ * CZ * MAIN : (x_ + 1) * CZ * MAIN], pm[...]) + mm_nt(rest, pr[x_])

    def norm(xw, at):
        total = None
        for n in range(Y):
            part = jnp.sum(xw[n].astype(F32), axis=-1, keepdims=True)
            total = part if total is None else total + part
        mean = total * (1.0 / N)
        total = None
        for n in range(Y):
            center = xw[n].astype(F32) - mean
            part = jnp.sum(center * center, axis=-1, keepdims=True)
            total = part if total is None else total + part
        inverse = lax.rsqrt(total * (1.0 / N) + EPS)
        stat[2 * at] = mean
        stat[2 * at + 1] = inverse
        slices = []
        for n in range(Y):
            normed = (xw[n].astype(F32) - mean) * inverse
            slices.append((normed * (1.0 + mod[3 * at + 1, n]) + mod[3 * at, n]).astype(BF))
        narrow(slices)

    K = X * CZ * MAIN

    def weight(b, k):
        return Wm[b, k].reshape(K, F), Wr[b * 4 + k]

    def project(b):
        for k in range(3):
            main, rest = weight(b, k)
            qkv[b, k] = (mm(mp[...], main) + mm(mpr[...], rest)).astype(BF)

    def spread(value):
        zero = jnp.zeros_like(value)
        return jnp.concatenate([jnp.where(head[h], value, zero) for h in range(H)], axis=0)

    def gather_heads(value):
        total = None
        for h in range(H):
            part = jnp.where(head[h], value[h * T : (h + 1) * T], 0.0)
            total = part if total is None else total + part
        return total.astype(BF)

    SCALE = HD ** (-0.5)

    def attend(b):
        scores = mm_nt(spread(qkv[b, 0]), qkv[b, 1]) * SCALE
        if b == 0:
            query_frame = lax.rem(iota((H * T, T), 0), T) // (G * Z)
            same = query_frame == iota((H * T, T), 1) // (G * Z)
            scores = jnp.where(same, scores, -1e30)
        weights = jnp.exp(scores - jnp.max(scores, axis=-1, keepdims=True))
        prob[b] = weights / jnp.sum(weights, axis=-1, keepdims=True)
        return gather_heads(mm(prob[b].astype(BF), qkv[b, 2]))

    def attend_back(b, grad):
        grads = spread(grad)
        likely = prob[b]
        grad_values = mm_tn(likely.astype(BF), grads).astype(BF)
        grad_likely = mm_nt(grads, qkv[b, 2])
        shift = grad_likely - jnp.sum(likely * grad_likely, axis=-1, keepdims=True)
        grad_scores = (likely * shift * SCALE).astype(BF)
        grad_query = gather_heads(mm(grad_scores, qkv[b, 1]))
        grad_keys = mm_tn(grad_scores, spread(qkv[b, 0])).astype(BF)
        return grad_query, grad_keys, grad_values

    def out_partial(b, flat, buf):
        main, rest = weight(b, 3)
        part = mm_nt(flat, main).astype(BF)
        part_rest = mm_nt(flat, rest).astype(BF)
        for n in range(Y):
            buf[n] = natural(part, part_rest, n)[:, :F].astype(BF)

    def grad_heads(b):
        main, rest = weight(b, 3)
        return (mm(mp[...], main) + mm(mpr[...], rest)).astype(BF)

    def in_partial(b, grads, xw, buf):
        part, part_rest = None, None
        for k in range(3):
            main, rest = weight(b, k)
            a, r = mm_nt(grads[k], main), mm_nt(grads[k], rest)
            part = a if part is None else part + a
            part_rest = r if part_rest is None else part_rest + r
        part, part_rest = part.astype(BF), part_rest.astype(BF)
        mean, inverse = stat[2 * b], stat[2 * b + 1]
        first, second = None, None
        slices = []
        for n in range(Y):
            value = natural(part, part_rest, n)
            slices.append(value)
            scaled = value[:, :F] * (1.0 + mod[3 * b + 1, n])
            normed = (xw[n].astype(F32) - mean) * inverse
            a = jnp.sum(scaled, axis=-1, keepdims=True)
            r = jnp.sum(scaled * normed, axis=-1, keepdims=True)
            first = a if first is None else first + a
            second = r if second is None else second + r
        spot = iota((1, FP), 1)
        for n in range(Y):
            value = jnp.where(spot == F, first, jnp.where(spot == F + 1, second, slices[n]))
            buf[n] = value.astype(BF)

    def in_finish(b, buf, xw, incoming):
        total = buf[0].astype(F32)
        for n in range(1, Y):
            total = total + buf[n].astype(F32)
        first = total[:, F : F + 1] * (1.0 / N)
        second = total[:, F + 1 : F + 2] * (1.0 / N)
        scaled = total[:, :F] * (1.0 + mod[3 * b + 1, y])
        normed = (xw[y].astype(F32) - stat[2 * b]) * stat[2 * b + 1]
        grad = stat[2 * b + 1] * (scaled - first - normed * second)
        return (incoming.astype(F32) + grad).astype(BF)

    def add_up(buf):
        total = buf[0].astype(F32)
        for n in range(1, Y):
            total = total + buf[n].astype(F32)
        return total

    def gated(b, value):
        return (mod[3 * b + 2, y] * value.astype(F32)).astype(BF)

    def wg_start(b, flat):
        main = mm_tn(mp[...], flat).astype(BF)
        rest = mm_tn(mpr[...], flat).astype(BF)
        wgp[b, :, :, :Z] = main.reshape(X, C, Z, MAIN, F)
        wgp[b, :, :, Z] = rest.reshape(X, C, Z * R2, F)
        send(wgp.at[b, :, 1 - c], wgc.at[b], names["wc%d" % b], sibling)

    def wg_second(b):
        recv(wgc.at[b], names["wc%d" % b])
        wgx[b] = (wgp[b, :, c].astype(F32) + wgc[b].astype(F32)).astype(BF)
        ex_send(lambda p: wgx.at[b, p], wgxr.at[b], names["wx%d" % b], X, x, dev_x)
        wgxr[b, x] = wgx[b, x]

    def wg_third(b):
        ex_wait(wgxr.at[b], names["wx%d" % b], X, x)
        total = wgxr[b, 0].astype(F32)
        for n in range(1, X):
            total = total + wgxr[b, n].astype(F32)
        total = total.astype(BF)
        for n in range(Z):
            wgz[b, n, 0] = total[n]
            wgz[b, n, 1] = total[Z]
        ex_send(
            lambda p: wgz.at[b, lax.rem(p, Z)], wgzr.at[b], names["wz%d" % b], ZG, zg, dev_zg
        )
        wgzr[b, zg] = wgz[b, z]

    def wg_end(b, ref):
        ex_wait(wgzr.at[b], names["wz%d" % b], ZG, zg)
        main = wgzr[b, 0, 0].astype(F32)
        rest = wgzr[b, 0, 1].astype(F32)
        for n in range(1, ZG):
            main = main + wgzr[b, n, 0].astype(F32)
            rest = rest + wgzr[b, n, 1].astype(F32)
        ref[:MAIN] = main
        at = iota((Z * R2, F), 0)
        for r in range(R2):
            ref[MAIN + r : MAIN + r + 1] = jnp.sum(
                jnp.where(at == z * R2 + r, rest, 0.0), axis=0, keepdims=True
            )

    z_chain(0)
    right, left = lax.rem(x + 1, X), lax.rem(x + X - 1, X)
    across = lax.rem(x + X // 2, X)

    def piece(x_, k):
        return Rb.at[x_, c] if k == 4 else Wm.at[0, k, x_, c]

    xp = names["xp0"]
    ahead, behind = (0, 1, 2, 3, 4), (2, 4, 0, 1, 3)
    for n in range(5):
        send(piece(x, ahead[n]), piece(x, ahead[n]), xp + ahead[n], dev_x(right))
        if X > 2:
            send(piece(x, behind[n]), piece(x, behind[n]), xp + 5 + behind[n], dev_x(left))

    def to_sibling(b, x_, n):
        send(Wm.at[b, :, x_, c], Wm.at[b, :, x_, c], names["sib%d" % b] + n, sibling)
        if b == 0:
            send(Rb.at[x_, c], Rb.at[x_, c], names["sib0"] + X + n, sibling)

    def from_sibling(b, x_, n):
        recv(Wm.at[b, :, x_, 1 - c], names["sib%d" % b] + n)
        if b == 0:
            recv(Rb.at[x_, 1 - c], names["sib0"] + X + n)

    to_sibling(0, x, 0)

    ex_wait(cot_b, names["cot_x"], G, g)
    z_put(cot_c.at[0], to_z(flatten(cot_b)))
    ex_send(lambda p: cot_c.at[0, p], cot_c.at[1], names["cot_z"], Z, z, dev_z)
    cot_c[1, z] = cot_c[0, z]

    ex_wait(xw_s, names["tok"], Y, y)
    norm(xw_s, 0)

    if X > 2:
        for k in (0, 1):
            recv(piece(left, k), xp + k)
            send(piece(left, k), piece(left, k), xp + 10 + k, dev_x(right))
            if k == 0:
                for m in (2, 4):
                    recv(piece(right, m), xp + 5 + m)
                    send(piece(right, m), piece(right, m), xp + 10 + m, dev_x(left))
        for k in (2, 3, 4):
            recv(piece(left, k), xp + k)
        to_sibling(0, left, 1)
        for k in (0, 1, 3):
            recv(piece(right, k), xp + 5 + k)
        send(piece(right, 3), piece(right, 3), xp + 13, dev_x(left))
        to_sibling(0, right, 2)
        z_chain(1)
        for k in range(5):
            recv(piece(across, k), xp + 10 + k)
        to_sibling(0, across, 3)
        from_sibling(0, x, 0)
        from_sibling(0, left, 1)
        from_sibling(0, right, 2)
        from_sibling(0, across, 3)
    else:
        for k in range(5):
            recv(piece(left, k), xp + k)
        to_sibling(0, left, 1)
        z_chain(1)
        from_sibling(0, x, 0)
        from_sibling(0, left, 1)
    for k in range(1, X):
        to_x = lax.rem(x + k, X)
        send(Wm.at[1, :, x, c], Wm.at[1, :, x, c], names["xp1"] + k, dev_x(to_x))
    to_sibling(1, x, 0)

    ex_wait(cot_c.at[1], names["cot_z"], Z, z)
    cot_t = flatten(cot_c.at[1])
    gw_t[y] = gated(1, cot_t)
    ex_send(lambda p: gw_t.at[y], gw_t, names["ggt"], Y, y, dev_y)

    n_rest = CZ * 8 * R2
    o = iota((n_rest, n_rest), 0)
    source = lax.rem(o // R2, CZ) * (8 * R2) + o // (CZ * R2) * R2 + lax.rem(o, R2)
    shuffle = (iota((n_rest, n_rest), 1) == source).astype(BF)
    for x_ in range(X):
        rest = mm(shuffle, Rb[x_].reshape(n_rest, F)).astype(BF)
        Wr[:, x_ * CZ * R2 : (x_ + 1) * CZ * R2] = rest.reshape(8, CZ * R2, F)

    project(0)
    flat_s[...] = attend(0)
    out_partial(0, flat_s[...], rs1_a)
    ex_send(lambda p: rs1_a.at[p], rs1_b, names["rs1"], Y, y, dev_y)
    rs1_b[y] = rs1_a[y]

    for k in range(1, X):
        x_ = lax.rem(x + X - k, X)
        recv(Wm.at[1, :, x_, c], names["xp1"] + k)
        to_sibling(1, x_, k)

    ex_wait(rs1_b, names["rs1"], Y, y)
    first = tok[...].astype(F32) + mod[2, y] * add_up(rs1_b)
    x_put(fst_a, to_groups(first.astype(BF)))
    ex_send(lambda p: fst_a.at[p], fst_b, names["fst_x"], G, g, dev_g)
    fst_b[g] = fst_a[g]

    from_sibling(1, x, 0)
    for k in range(1, X):
        from_sibling(1, lax.rem(x + X - k, X), k)
    ex_wait(gw_t, names["ggt"], Y, y)

    ex_wait(fst_b, names["fst_x"], G, g)
    z_put(fst_c, to_z(flatten(fst_b)))
    ex_send(lambda p: fst_c.at[p], fst_d, names["fst_z"], Z, z, dev_z)
    fst_d[z] = fst_c[z]

    ex_wait(fst_d, names["fst_z"], Z, z)
    xw_t[y] = flatten(fst_d)
    ex_send(lambda p: xw_t.at[y], xw_t, names["fst"], Y, y, dev_y)

    narrow([gw_t[n] for n in range(Y)])
    grad_t = grad_heads(1)

    ex_wait(xw_t, names["fst"], Y, y)
    norm(xw_t, 1)
    project(1)
    flat_t = attend(1)
    grads = attend_back(1, grad_t)
    in_partial(1, grads, xw_t, rsg_a)
    ex_send(lambda p: rsg_a.at[p], rsg_b, names["rsg"], Y, y, dev_y)
    rsg_b[y] = rsg_a[y]

    out_partial(1, flat_t, rsp_a)
    ex_send(lambda p: rsp_a.at[p], rsp_b, names["rsp"], Y, y, dev_y)
    rsp_b[y] = rsp_a[y]

    ex_wait(rsg_b, names["rsg"], Y, y)
    z_put(fg_a, in_finish(1, rsg_b, xw_t, cot_t))
    ex_send(lambda p: fg_a.at[p], fg_b, names["fg_z"], Z, z, dev_z)
    fg_b[z] = fg_a[z]

    narrow([gw_t[n] for n in range(Y)])
    wg_start(1, flat_t)

    ex_wait(fg_b, names["fg_z"], Z, z)
    x_put(fg_c, from_z(flatten(fg_b)))
    ex_send(lambda p: fg_c.at[p], fg_d, names["fg_x"], G, g, dev_g)
    fg_d[g] = fg_c[g]

    ex_wait(rsp_b, names["rsp"], Y, y)
    second = xw_t[y].astype(F32) + mod[5, y] * add_up(rsp_b)
    z_put(out_a, second.astype(BF))
    ex_send(lambda p: out_a.at[p], out_b, names["out_z"], Z, z, dev_z)
    out_b[z] = out_a[z]

    ex_wait(fg_d, names["fg_x"], G, g)
    fg_e[...] = from_groups(flatten(fg_d))
    gw_s[y] = gated(0, fg_e[...])
    ex_send(lambda p: gw_s.at[y], gw_s, names["ggs"], Y, y, dev_y)

    wg_second(1)
    ex_wait(out_b, names["out_z"], Z, z)
    x_put(out_c, from_z(flatten(out_b)))
    ex_send(lambda p: out_c.at[p], out_d, names["out_x"], G, g, dev_g)
    out_d[g] = out_c[g]

    ex_wait(gw_s, names["ggs"], Y, y)
    narrow([gw_s[n] for n in range(Y)])
    wg_start(0, flat_s[...])
    grad_s = grad_heads(0)
    wg_third(1)
    wg_second(0)
    grads = attend_back(0, grad_s)
    wg_third(0)
    in_partial(0, grads, xw_s, rsf_a)
    ex_send(lambda p: rsf_a.at[p], rsf_b, names["rsf"], Y, y, dev_y)
    rsf_b[y] = rsf_a[y]

    ex_wait(out_d, names["out_x"], G, g)
    out[...] = from_groups(flatten(out_d))
    wg_end(1, wg_t)
    ex_wait(rsf_b, names["rsf"], Y, y)
    igrad[...] = in_finish(0, rsf_b, xw_s, fg_e[...])
    wg_end(0, wg_s)
    for copy in sent:
        copy.wait_send()


def on_device(sizes, tokens, modulation, qkv_s, out_s, qkv_t, out_t, cotangent):
    DP, S, Y = sizes
    frames, patches, F = tokens.shape[1:]
    T = frames * patches
    X, C = Y, 2
    Z = S // (X * C)
    G = X * C
    H = F // HD
    rows = out_s.shape[0]
    R2 = rows - MAIN
    FP = (F + 2 + 127) // 128 * 128
    dims = (X, C, Z, Y, DP, T, F, H, R2)
    names, count = layout(X, C, Z, Y, DP)

    def joined(qkv, out):
        return jnp.concatenate([qkv.transpose(1, 0, 2), out[None]], axis=0)

    weights = jnp.stack([joined(qkv_s, out_s), joined(qkv_t, out_t)])
    wmain = weights[:, :, :MAIN]
    wrest = weights[:, :, MAIN:].reshape(8 * R2, F)
    mod = modulation.reshape(6, Y, 1, F)

    K, KR = X * C * Z * MAIN, X * C * Z * R2
    xs, zs = pltpu.VMEM((G, 2 * Z, F), BF), pltpu.VMEM((Z, 2 * G, F), BF)
    wide, padded = pltpu.VMEM((Y, T, F), BF), pltpu.VMEM((Y, T, FP), BF)
    scratch = [
        pltpu.SemaphoreType.DMA((count,)),
        pltpu.SemaphoreType.DMA((count,)),
        pltpu.VMEM((FP, C * Z * MAIN), BF),
        pltpu.VMEM((X, FP, KR), BF),
        wide, wide, wide, wide,
        pltpu.VMEM((2, 4, X, C, Z, MAIN, F), BF),
        pltpu.VMEM((X, C, Z, 8 * R2, F), BF),
        pltpu.VMEM((8, KR, F), BF),
        xs, xs, pltpu.VMEM((2, Z, 2 * G, F), BF),
        xs, xs, zs, zs,
        zs, zs, xs, xs, pltpu.VMEM((T, F), BF),
        zs, zs, xs, xs,
        pltpu.VMEM((T, K), BF),
        pltpu.VMEM((T, KR), BF),
        pltpu.VMEM((2, 3, T, F), BF),
        pltpu.VMEM((2, H * T, T), F32),
        pltpu.VMEM((T, F), BF),
        pltpu.VMEM((4, T, 1), F32),
        wide, wide, padded, padded, wide, wide, padded, padded,
        pltpu.VMEM((2, X, C, Z + 1, MAIN, F), BF),
        pltpu.VMEM((2, X, Z + 1, MAIN, F), BF),
        pltpu.VMEM((2, X, Z + 1, MAIN, F), BF),
        pltpu.VMEM((2, X, Z + 1, MAIN, F), BF),
        pltpu.VMEM((2, Z, 2, MAIN, F), BF),
        pltpu.VMEM((2, DP * Z, 2, MAIN, F), BF),
    ]
    vmem = pl.BlockSpec(memory_space=pltpu.VMEM)
    out, igrad, wg_s, wg_t = pl.pallas_call(
        functools.partial(kernel, dims, names),
        out_shape=(
            jax.ShapeDtypeStruct((T, F), BF),
            jax.ShapeDtypeStruct((T, F), BF),
            jax.ShapeDtypeStruct((rows, F), F32),
            jax.ShapeDtypeStruct((rows, F), F32),
        ),
        in_specs=[vmem] * 5,
        out_specs=(vmem,) * 4,
        scratch_shapes=scratch,
        compiler_params=pltpu.CompilerParams(
            collective_id=0, has_side_effects=True, vmem_limit_bytes=56 * 2**20
        ),
    )(tokens.reshape(T, F), cotangent.reshape(T, F), mod, wmain, wrest)
    shape = (1, frames, patches, F)
    return out.reshape(shape), igrad.reshape(shape), wg_s, wg_t


def solution(mesh):
    sizes = tuple(mesh.shape[a] for a in ("dp", "seq", "tp"))
    placed = (
        P("dp", "seq", None, "tp"),
        P("dp", None, None),
        P("seq", None, "tp"),
        P("seq", "tp"),
        P("seq", None, "tp"),
        P("seq", "tp"),
        P("dp", "seq", None, "tp"),
    )
    return jax.shard_map(
        functools.partial(on_device, sizes),
        mesh=mesh,
        in_specs=placed,
        out_specs=(
            P("dp", "seq", None, "tp"),
            P("dp", "seq", None, "tp"),
            P("seq", "tp"),
            P("seq", "tp"),
        ),
        check_vma=False,
    )
```

time: 1160 us -> 174 us (0.15)
  waiting for transfers between devices: 698 us -> 0 us
  blocking collectives: 338 us -> 0 us
  Pallas kernels: 0 us -> 162 us
  starting transfers between devices: 44.3 us -> 0 us
  matrix products: 26.3 us -> 0 us
  local copies, waits for them, and re-layouts: 25.6 us -> 6.64 us
  between operations: 15.1 us -> 0.68 us
    psum x3 -> x0, waiting for transfers between devices: 461 us -> none  [the longest x1 358 us: on_device(): lax.psum((weight_spatial, weight_temporal), ('dp', 'seq'))]
    all_gather x6 -> x0, blocking collectives: 306 us -> none  [the longest x1 135 us: on_device(): lax.all_gather(out_spatial, 'seq', axis=0, tiled=True)]
    pallas_call x0 -> x1, Pallas kernels: none -> 162 us  [on_device(): pl.pallas_call(functools.partial(kernel, dims, names), out_shape=(jax.Sha...]
    all_gather x2 -> x0, waiting for transfers between devices: 114 us -> none  [the longest x1 114 us: on_device(): lax.all_gather(qkv_temporal, 'seq', axis=0, tiled=True)]
    all_to_all x7 -> x0, waiting for transfers between devices: 82.7 us -> none  [the longest x1 14.3 us: heads_forward(): lax.all_to_all(values, 'seq', split_axis=1, concat_axis=0, tiled=True)]
    all_to_all x7 -> x0, starting transfers between devices: 44 us -> none  [the longest x1 7.4 us: heads_forward(): lax.all_to_all(keys, 'seq', split_axis=1, concat_axis=0, tiled=True)]
    unnamed x9 -> x0, waiting for transfers between devices: 41.3 us -> none
    all_to_all x1 -> x0, blocking collectives: 32.7 us -> none  [heads_backward(): lax.all_to_all(grad_out, 'seq', split_axis=1, concat_axis=0, tiled=True)]
  transfers between devices with their start and end apart: 14 -> 0, of which waited for: 12 -> 0; matrix products, arithmetic and copies ran while one was open for 1% -> 0% of each run, Pallas kernels for 0% -> 0%
where the time goes in v1:
time: 174 us; the launch traced here: 170 us
  Pallas kernels  162 us (93%)
  local copies, waits for them, and re-layouts  6.64 us (4%)
    pallas_call x1, Pallas kernels, on_device(): pl.pallas_call(functools.partial(kernel, dims, names), out_shape=(jax.Sha...  162 us
    unnamed x20, local copies, waits for them, and re-layouts  5.29 us

profile of v1, /device:TPU:1, one launch (start us, length us, event | category | flops | bytes accessed | tf_op | source)
XLA Modules:
  0.0 170.5 jit_solution(6483653885285625151)
XLA Ops:
  0.6 0.0 copy-start.1
  0.6 0.8 reduce
  1.5 0.7 reshape.28.mod
  2.2 0.0 copy-done.1
  2.2 0.0 copy-start.2
  2.2 0.8 copy-done.2
  3.0 0.0 copy-start.5
  3.0 0.0 copy-start.6
  3.0 0.7 copy-done.5
  3.7 0.0 copy-done.6
  3.8 0.7 fusion.wmain
  4.5 0.6 reshape.29.wrest
  5.1 161.6 %shard_map.102 = (bf16[128,288]{1,0:T(8,128)(2,1)}, bf16[128,288]{1,0:T(8,128)(2,1)}, f32[18,288]{1,0:T(8,128)}, f32[18,288]{1,0:T(8,128)}) custom-call(bf16[128,288]{1,0:T(8,128)(2,1)} %bitcast.20, bf16[128,288]{1,0:T(8,128)(2,1)} %bitcast.21, f32[6,4,1,288]{3,2,1,0:T(1,128)} %reshape.28.mod, bf16[2,4,16,288]{3,2,1,0:T(8,128)(2,1)} %fusion.wmain, ...), custom_call_target="tpu_custom_call" | custom-call | tf_op jit(solution)/shard_map/pallas_call | solution.py:647
  166.7 0.0 copy-start
  166.7 1.6 copy.21
  168.3 0.0 copy-done
  168.3 0.0 copy-start.4
  168.3 0.6 copy.22
  169.0 0.1 copy-done.4
  169.1 0.0 copy-start.3
  169.1 0.6 copy.23
  169.7 0.2 copy-done.3
  169.9 0.6 copy.24
  (4 shorter events, 0.1 us)
Async XLA Ops:
  0.6 1.6 copy-start.1
  2.2 0.8 copy-start.2
  3.0 0.7 copy-start.5
  3.0 0.7 copy-start.6
  166.7 1.6 copy-start
  168.3 0.8 copy-start.4
  169.1 0.8 copy-start.3

commit v2 on v1

--- a/solution.py
+++ b/solution.py
@@ -51,11 +51,10 @@
         names[name] = s.take(G)
     for name in ("cot_z", "fst_z", "fg_z", "out_z"):
         names[name] = s.take(Z)
-    for name in ("zu0", "zd0", "zu0r", "zd0r", "zu1", "zd1"):
+    for name in ("zu0", "zd0", "zu1", "zd1", "xr0", "xl0", "xo0"):
         names[name] = s.take(Z)
-    names["xp0"] = s.take(15)
+    names["sib0"] = s.take(X * Z)
     names["xp1"] = s.take(X)
-    names["sib0"] = s.take(2 * X)
     names["sib1"] = s.take(X)
     for b in (0, 1):
         names["wc%d" % b] = s.take(1)
@@ -64,12 +63,12 @@
     return names, s.count
 
 
-def kernel(dims, names, tok, cot, mod, wmain, wrest, out, igrad, wg_s, wg_t, *refs):
-    X, C, Z, Y, DP, T, F, H, R2 = dims
+def kernel(dims, names, tok, cot, mods, wown, wown_t, out, igrad, wg_s, wg_t, *refs):
+    X, C, Z, Y, DP, T, F, FP, H, R2 = dims
     G = X * C
     N = Y * F
     (
-        ssem, rsem, pm, pr, xw_s, xw_t, gw_t, gw_s, Wm, Rb, Wr,
+        ssem, rsem, mod, pm, pr, xw_s, xw_t, gw_t, gw_s, Ws, Wt, Wr, cotp,
         cot_a, cot_b, cot_c, fst_a, fst_b, fst_c, fst_d, fg_a, fg_b, fg_c, fg_d, fg_e,
         out_a, out_b, out_c, out_d,
         mp, mpr, qkv, prob, flat_s, stat,
@@ -142,46 +141,83 @@
         pl.semaphore_signal(barrier, inc=1, device_id=peer, device_id_type=MESH)
     pl.semaphore_wait(barrier, len(peers))
 
-    ex_send(lambda p: tok, xw_s, names["tok"], Y, y, dev_y)
-
     up, down = dev_zg(lax.rem(zg + 1, ZG)), dev_zg(lax.rem(zg + ZG - 1, ZG))
+    right, left = lax.rem(x + 1, X), lax.rem(x + X - 1, X)
+    across = lax.rem(x + X // 2, X)
     nup = Z // 2
     ndown = Z - 1 - nup
 
     def w_slot(b, x_, c_, z_):
-        return Wm.at[b, :, x_, c_, z_]
-
-    def z_hop(step, first, b, device, sem, semr):
+        return (Wt if b else Ws).at[:, x_, c_, z_]
+
+    def z_hop(step, first, b):
         z_ = lax.rem(z + first * step + Z * Z, Z)
-        src = wmain.at[b] if step == 0 else w_slot(b, x, c, z_)
-        send(src, w_slot(b, x, c, z_), sem + step, device)
-        if b == 0:
-            src = wrest if step == 0 else Rb.at[x, c, z_]
-            send(src, Rb.at[x, c, z_], semr + step, device)
-
-    def z_take(step, first, b, sem, semr):
+        slot = w_slot(b, x, c, z_)
+        src = (wown_t if b else wown) if step == 0 else slot
+        send(src, slot, names["z%s%d" % ("u" if first < 0 else "d", b)] + step, up if first < 0 else down)
+
+    def z_take(step, first, b):
         z_ = lax.rem(z + first * (step + 1) + Z * Z, Z)
-        recv(w_slot(b, x, c, z_), sem + step)
-        if b == 0:
-            recv(Rb.at[x, c, z_], semr + step)
+        recv(w_slot(b, x, c, z_), names["z%s%d" % ("u" if first < 0 else "d", b)] + step)
+        return z_
 
     def z_start(b):
         if nup:
-            z_hop(0, -1, b, up, names["zu%d" % b], names["zu0r"])
+            z_hop(0, -1, b)
         if ndown:
-            z_hop(0, 1, b, down, names["zd%d" % b], names["zd0r"])
-
-    def z_chain(b):
+            z_hop(0, 1, b)
+
+    def z_chain(b, arrived):
         for step in range(nup):
-            z_take(step, -1, b, names["zu%d" % b], names["zu0r"])
+            z_ = z_take(step, -1, b)
             if step + 1 < nup:
-                z_hop(step + 1, -1, b, up, names["zu%d" % b], names["zu0r"])
+                z_hop(step + 1, -1, b)
+            arrived(2 * step + 1, z_)
             if step < ndown:
-                z_take(step, 1, b, names["zd%d" % b], names["zd0r"])
+                z_ = z_take(step, 1, b)
                 if step + 1 < ndown:
-                    z_hop(step + 1, 1, b, down, names["zd%d" % b], names["zd0r"])
+                    z_hop(step + 1, 1, b)
+                arrived(2 * step + 2, z_)
+
+    def order(i):
+        return lax.rem(z + (-(i + 1) // 2 if i % 2 else i // 2) + Z, Z)
+
+    def x_hop(i, own=False):
+        slot = w_slot(0, x, c, order(i))
+        src = wown if own else slot
+        send(src, slot, names["xr0"] + i, dev_x(right))
+        if X > 2:
+            send(src, slot, names["xl0"] + i, dev_x(left))
+        send(src, w_slot(0, x, c, order(i)), names["sib0"] + i, sibling)
+
+    def x_take(i):
+        recv(w_slot(0, left, c, order(i)), names["xr0"] + i)
+        if X > 2:
+            slot = w_slot(0, left, c, order(i))
+            if i % 2 == 0:
+                send(slot, slot, names["xo0"] + i, dev_x(right))
+            send(slot, slot, names["sib0"] + Z + i, sibling)
+            slot = w_slot(0, right, c, order(i))
+            recv(slot, names["xl0"] + i)
+            if i % 2 == 1:
+                send(slot, slot, names["xo0"] + i, dev_x(left))
+            send(slot, slot, names["sib0"] + 2 * Z + i, sibling)
+        else:
+            slot = w_slot(0, left, c, order(i))
+            send(slot, slot, names["sib0"] + Z + i, sibling)
+
+    def x_last(i):
+        slot = w_slot(0, across, c, order(i))
+        recv(slot, names["xo0"] + i)
+        send(slot, slot, names["sib0"] + 3 * Z + i, sibling)
 
     z_start(0)
+    x_hop(0, True)
+    xw_s[y] = jnp.zeros((T, FP), BF)
+    xw_s[y, :, :F] = tok[...]
+    ex_send(lambda p: xw_s.at[y], xw_s, names["tok"], Y, y, dev_y)
+    cotp[...] = jnp.zeros((T, FP), BF)
+    cotp[:, :F] = cot[...]
 
     row = iota((T, T), 0)
     col = iota((T, T), 1)
@@ -204,25 +240,26 @@
         return swap_rows(value, lax.rem(row, Z) * (2 * G) + row // Z)
 
     def x_put(buf, value):
-        buf[...] = value.reshape(G, 2 * Z, F)
+        buf[...] = value.reshape(G, 2 * Z, FP)
 
     def z_put(buf, value):
-        buf[...] = value.reshape(Z, 2 * G, F)
+        buf[...] = value.reshape(Z, 2 * G, FP)
 
     def flatten(buf):
-        return buf[...].reshape(T, F)
-
-    x_put(cot_a, to_groups(cot[...]))
+        return buf[...].reshape(T, FP)
+
+    x_put(cot_a, to_groups(cotp[...]))
     ex_send(lambda p: cot_a.at[p], cot_b, names["cot_x"], G, g, dev_g)
-    z_start(1)
     cot_b[g] = cot_a[g]
-    xw_s[y] = tok[...]
-    for b in (0, 1):
-        for k in range(4):
-            Wm[b, k, x, c, z] = wmain[b, k]
-    Rb[x, c, z] = wrest[...]
-
-    FP = pm.shape[0]
+    for k in range(5):
+        Ws[k, x, c, z] = wown[k]
+    for k in range(4):
+        Wt[k, x, c, z] = wown_t[k]
+    mod[...] = jnp.zeros((6, Y, 1, FP), F32)
+    for i in range(6):
+        for n in range(Y):
+            mod[i, n, :, :F] = mods[i : i + 1, n * F : (n + 1) * F]
+
     CZ = C * Z
     j = iota((FP, CZ * MAIN), 1)
     target = (lax.rem(j // MAIN, Z) * C + j // (Z * MAIN)) * (MAIN + R2) + lax.rem(j, MAIN)
@@ -234,15 +271,16 @@
     for x_ in range(X):
         pr[x_] = (hit & (j // (CZ * R2) == x_)).astype(BF)
 
-    lane = iota((1, F), 1)
+    lane = iota((1, FP), 1)
+    inside = lane < F
     head = [(lane >= h * HD) & (lane < (h + 1) * HD) for h in range(H)]
 
     def narrow(slices):
         rest = None
         for x_ in range(X):
             part = slices[x_]
-            mp[:, x_ * CZ * MAIN : (x_ + 1) * CZ * MAIN] = mm(part, pm[:F]).astype(BF)
-            more = mm(part, pr[x_, :F])
+            mp[:, x_ * CZ * MAIN : (x_ + 1) * CZ * MAIN] = mm(part, pm[...]).astype(BF)
+            more = mm(part, pr[x_])
             rest = more if rest is None else rest + more
         mpr[...] = rest.astype(BF)
 
@@ -257,7 +295,7 @@
         mean = total * (1.0 / N)
         total = None
         for n in range(Y):
-            center = xw[n].astype(F32) - mean
+            center = jnp.where(inside, xw[n].astype(F32) - mean, 0.0)
             part = jnp.sum(center * center, axis=-1, keepdims=True)
             total = part if total is None else total + part
         inverse = lax.rsqrt(total * (1.0 / N) + EPS)
@@ -272,7 +310,7 @@
     K = X * CZ * MAIN
 
     def weight(b, k):
-        return Wm[b, k].reshape(K, F), Wr[b * 4 + k]
+        return (Wt if b else Ws)[k].reshape(K, FP), Wr[b * 4 + k]
 
     def project(b):
         for k in range(3):
@@ -318,7 +356,7 @@
         part = mm_nt(flat, main).astype(BF)
         part_rest = mm_nt(flat, rest).astype(BF)
         for n in range(Y):
-            buf[n] = natural(part, part_rest, n)[:, :F].astype(BF)
+            buf[n] = natural(part, part_rest, n).astype(BF)
 
     def grad_heads(b):
         main, rest = weight(b, 3)
@@ -338,15 +376,14 @@
         for n in range(Y):
             value = natural(part, part_rest, n)
             slices.append(value)
-            scaled = value[:, :F] * (1.0 + mod[3 * b + 1, n])
+            scaled = value * (1.0 + mod[3 * b + 1, n])
             normed = (xw[n].astype(F32) - mean) * inverse
             a = jnp.sum(scaled, axis=-1, keepdims=True)
             r = jnp.sum(scaled * normed, axis=-1, keepdims=True)
             first = a if first is None else first + a
             second = r if second is None else second + r
-        spot = iota((1, FP), 1)
         for n in range(Y):
-            value = jnp.where(spot == F, first, jnp.where(spot == F + 1, second, slices[n]))
+            value = jnp.where(lane == F, first, jnp.where(lane == F + 1, second, slices[n]))
             buf[n] = value.astype(BF)
 
     def in_finish(b, buf, xw, incoming):
@@ -355,10 +392,10 @@
             total = total + buf[n].astype(F32)
         first = total[:, F : F + 1] * (1.0 / N)
         second = total[:, F + 1 : F + 2] * (1.0 / N)
-        scaled = total[:, :F] * (1.0 + mod[3 * b + 1, y])
+        scaled = total * (1.0 + mod[3 * b + 1, y])
         normed = (xw[y].astype(F32) - stat[2 * b]) * stat[2 * b + 1]
         grad = stat[2 * b + 1] * (scaled - first - normed * second)
-        return (incoming.astype(F32) + grad).astype(BF)
+        return jnp.where(inside, incoming.astype(F32) + grad, 0.0).astype(BF)
 
     def add_up(buf):
         total = buf[0].astype(F32)
@@ -369,11 +406,18 @@
     def gated(b, value):
         return (mod[3 * b + 2, y] * value.astype(F32)).astype(BF)
 
+    FULL = FP - 128
+    WP = 128 - (F - FULL)
+
+    def shift_lanes(n):
+        a, b = iota((FP, 128), 0), iota((FP, 128), 1)
+        return ((a - n * WP == b - (128 - WP)) & (b >= 128 - WP)).astype(BF)
+
     def wg_start(b, flat):
         main = mm_tn(mp[...], flat).astype(BF)
         rest = mm_tn(mpr[...], flat).astype(BF)
-        wgp[b, :, :, :Z] = main.reshape(X, C, Z, MAIN, F)
-        wgp[b, :, :, Z] = rest.reshape(X, C, Z * R2, F)
+        wgp[b, :, :, :Z] = main.reshape(X, C, Z, MAIN, FP)
+        wgp[b, :, :, Z] = rest.reshape(X, C, Z * R2, FP)
         send(wgp.at[b, :, 1 - c], wgc.at[b], names["wc%d" % b], sibling)
 
     def wg_second(b):
@@ -388,9 +432,17 @@
         for n in range(1, X):
             total = total + wgxr[b, n].astype(F32)
         total = total.astype(BF)
-        for n in range(Z):
-            wgz[b, n, 0] = total[n]
-            wgz[b, n, 1] = total[Z]
+        main, rest = total[:Z].reshape(Z * MAIN, FP), total[Z]
+        wgz[b, :, :, :FULL] = main[:, :FULL].reshape(Z, MAIN, FULL)
+        tail = main[:, FULL:].astype(F32)
+        for n in range(F // WP):
+            pick = shift_lanes(n)
+            o = iota((Z * MAIN, Z * R2), 0)
+            slot = lax.rem(o, MAIN) - n * R2
+            rows = (o // MAIN) * R2 + slot == iota((Z * MAIN, Z * R2), 1)
+            rows = (rows & (slot >= 0) & (slot < R2)).astype(BF)
+            tail = tail + mm(rows, mm(rest, pick).astype(BF))
+        wgz[b, :, :, FULL:] = tail.astype(BF).reshape(Z, MAIN, 128)
         ex_send(
             lambda p: wgz.at[b, lax.rem(p, Z)], wgzr.at[b], names["wz%d" % b], ZG, zg, dev_zg
         )
@@ -398,43 +450,24 @@
 
     def wg_end(b, ref):
         ex_wait(wgzr.at[b], names["wz%d" % b], ZG, zg)
-        main = wgzr[b, 0, 0].astype(F32)
-        rest = wgzr[b, 0, 1].astype(F32)
+        total = wgzr[b, 0].astype(F32)
         for n in range(1, ZG):
-            main = main + wgzr[b, n, 0].astype(F32)
-            rest = rest + wgzr[b, n, 1].astype(F32)
-        ref[:MAIN] = main
-        at = iota((Z * R2, F), 0)
-        for r in range(R2):
-            ref[MAIN + r : MAIN + r + 1] = jnp.sum(
-                jnp.where(at == z * R2 + r, rest, 0.0), axis=0, keepdims=True
-            )
-
-    z_chain(0)
-    right, left = lax.rem(x + 1, X), lax.rem(x + X - 1, X)
-    across = lax.rem(x + X // 2, X)
-
-    def piece(x_, k):
-        return Rb.at[x_, c] if k == 4 else Wm.at[0, k, x_, c]
-
-    xp = names["xp0"]
-    ahead, behind = (0, 1, 2, 3, 4), (2, 4, 0, 1, 3)
-    for n in range(5):
-        send(piece(x, ahead[n]), piece(x, ahead[n]), xp + ahead[n], dev_x(right))
-        if X > 2:
-            send(piece(x, behind[n]), piece(x, behind[n]), xp + 5 + behind[n], dev_x(left))
-
-    def to_sibling(b, x_, n):
-        send(Wm.at[b, :, x_, c], Wm.at[b, :, x_, c], names["sib%d" % b] + n, sibling)
-        if b == 0:
-            send(Rb.at[x_, c], Rb.at[x_, c], names["sib0"] + X + n, sibling)
-
-    def from_sibling(b, x_, n):
-        recv(Wm.at[b, :, x_, 1 - c], names["sib%d" % b] + n)
-        if b == 0:
-            recv(Rb.at[x_, 1 - c], names["sib0"] + X + n)
-
-    to_sibling(0, x, 0)
+            total = total + wgzr[b, n].astype(F32)
+        ref[:MAIN, :FULL] = total[:, :FULL]
+        tail = total[:, FULL:]
+        ref[:MAIN, FULL:] = tail[:, : F - FULL]
+        for n in range(F // WP):
+            ref[MAIN : MAIN + R2, n * WP : (n + 1) * WP] = tail[n * R2 : (n + 1) * R2, 128 - WP :]
+
+    late = 2
+
+    def arrived(i, z_):
+        x_hop(i)
+        if i >= late:
+            x_take(i - late)
+
+    z_chain(0, arrived)
+    z_start(1)
 
     ex_wait(cot_b, names["cot_x"], G, g)
     z_put(cot_c.at[0], to_z(flatten(cot_b)))
@@ -444,40 +477,26 @@
     ex_wait(xw_s, names["tok"], Y, y)
     norm(xw_s, 0)
 
+    for i in range(Z - late, Z):
+        x_take(i)
+    z_chain(1, lambda i, z_: None)
     if X > 2:
-        for k in (0, 1):
-            recv(piece(left, k), xp + k)
-            send(piece(left, k), piece(left, k), xp + 10 + k, dev_x(right))
-            if k == 0:
-                for m in (2, 4):
-                    recv(piece(right, m), xp + 5 + m)
-                    send(piece(right, m), piece(right, m), xp + 10 + m, dev_x(left))
-        for k in (2, 3, 4):
-            recv(piece(left, k), xp + k)
-        to_sibling(0, left, 1)
-        for k in (0, 1, 3):
-            recv(piece(right, k), xp + 5 + k)
-        send(piece(right, 3), piece(right, 3), xp + 13, dev_x(left))
-        to_sibling(0, right, 2)
-        z_chain(1)
-        for k in range(5):
-            recv(piece(across, k), xp + 10 + k)
-        to_sibling(0, across, 3)
-        from_sibling(0, x, 0)
-        from_sibling(0, left, 1)
-        from_sibling(0, right, 2)
-        from_sibling(0, across, 3)
-    else:
-        for k in range(5):
-            recv(piece(left, k), xp + k)
-        to_sibling(0, left, 1)
-        z_chain(1)
-        from_sibling(0, x, 0)
-        from_sibling(0, left, 1)
+        for i in range(Z):
+            x_last(i)
+    for i in range(Z):
+        recv(w_slot(0, x, 1 - c, order(i)), names["sib0"] + i)
+        recv(w_slot(0, left, 1 - c, order(i)), names["sib0"] + Z + i)
+        if X > 2:
+            recv(w_slot(0, right, 1 - c, order(i)), names["sib0"] + 2 * Z + i)
+            recv(w_slot(0, across, 1 - c, order(i)), names["sib0"] + 3 * Z + i)
+
+    def to_sibling(x_, n):
+        send(Wt.at[:, x_, c], Wt.at[:, x_, c], names["sib1"] + n, sibling)
+
     for k in range(1, X):
         to_x = lax.rem(x + k, X)
-        send(Wm.at[1, :, x, c], Wm.at[1, :, x, c], names["xp1"] + k, dev_x(to_x))
-    to_sibling(1, x, 0)
+        send(Wt.at[:, x, c], Wt.at[:, x, c], names["xp1"] + k, dev_x(to_x))
+    to_sibling(x, 0)
 
     ex_wait(cot_c.at[1], names["cot_z"], Z, z)
     cot_t = flatten(cot_c.at[1])
@@ -489,8 +508,8 @@
     source = lax.rem(o // R2, CZ) * (8 * R2) + o // (CZ * R2) * R2 + lax.rem(o, R2)
     shuffle = (iota((n_rest, n_rest), 1) == source).astype(BF)
     for x_ in range(X):
-        rest = mm(shuffle, Rb[x_].reshape(n_rest, F)).astype(BF)
-        Wr[:, x_ * CZ * R2 : (x_ + 1) * CZ * R2] = rest.reshape(8, CZ * R2, F)
+        rest = mm(shuffle, Ws[4, x_].reshape(n_rest, FP)).astype(BF)
+        Wr[:, x_ * CZ * R2 : (x_ + 1) * CZ * R2] = rest.reshape(8, CZ * R2, FP)
 
     project(0)
     flat_s[...] = attend(0)
@@ -500,18 +519,17 @@
 
     for k in range(1, X):
         x_ = lax.rem(x + X - k, X)
-        recv(Wm.at[1, :, x_, c], names["xp1"] + k)
-        to_sibling(1, x_, k)
+        recv(Wt.at[:, x_, c], names["xp1"] + k)
+        to_sibling(x_, k)
 
     ex_wait(rs1_b, names["rs1"], Y, y)
-    first = tok[...].astype(F32) + mod[2, y] * add_up(rs1_b)
+    first = xw_s[y].astype(F32) + mod[2, y] * add_up(rs1_b)
     x_put(fst_a, to_groups(first.astype(BF)))
     ex_send(lambda p: fst_a.at[p], fst_b, names["fst_x"], G, g, dev_g)
     fst_b[g] = fst_a[g]
 
-    from_sibling(1, x, 0)
-    for k in range(1, X):
-        from_sibling(1, lax.rem(x + X - k, X), k)
+    for k in range(X):
+        recv(Wt.at[:, lax.rem(x + X - k, X), 1 - c], names["sib1"] + k)
     ex_wait(gw_t, names["ggt"], Y, y)
 
     ex_wait(fst_b, names["fst_x"], G, g)
@@ -582,10 +600,10 @@
     rsf_b[y] = rsf_a[y]
 
     ex_wait(out_d, names["out_x"], G, g)
-    out[...] = from_groups(flatten(out_d))
+    out[...] = from_groups(flatten(out_d))[:, :F]
     wg_end(1, wg_t)
     ex_wait(rsf_b, names["rsf"], Y, y)
-    igrad[...] = in_finish(0, rsf_b, xw_s, fg_e[...])
+    igrad[...] = in_finish(0, rsf_b, xw_s, fg_e[...])[:, :F]
     wg_end(0, wg_s)
     for copy in sent:
         copy.wait_send()
@@ -602,46 +620,49 @@
     rows = out_s.shape[0]
     R2 = rows - MAIN
     FP = (F + 2 + 127) // 128 * 128
-    dims = (X, C, Z, Y, DP, T, F, H, R2)
+    dims = (X, C, Z, Y, DP, T, F, FP, H, R2)
     names, count = layout(X, C, Z, Y, DP)
 
     def joined(qkv, out):
-        return jnp.concatenate([qkv.transpose(1, 0, 2), out[None]], axis=0)
-
-    weights = jnp.stack([joined(qkv_s, out_s), joined(qkv_t, out_t)])
-    wmain = weights[:, :, :MAIN]
-    wrest = weights[:, :, MAIN:].reshape(8 * R2, F)
-    mod = modulation.reshape(6, Y, 1, F)
+        both = jnp.concatenate([qkv.transpose(1, 0, 2), out[None]], axis=0)
+        return jnp.pad(both, ((0, 0), (0, 0), (0, FP - F)))
+
+    first, second = joined(qkv_s, out_s), joined(qkv_t, out_t)
+    rest = jnp.concatenate([first[:, MAIN:], second[:, MAIN:]]).reshape(1, 8 * R2, FP)
+    wown = jnp.concatenate([first[:, :MAIN], rest])
+    wown_t = second[:, :MAIN]
 
     K, KR = X * C * Z * MAIN, X * C * Z * R2
-    xs, zs = pltpu.VMEM((G, 2 * Z, F), BF), pltpu.VMEM((Z, 2 * G, F), BF)
-    wide, padded = pltpu.VMEM((Y, T, F), BF), pltpu.VMEM((Y, T, FP), BF)
+    xs, zs = pltpu.VMEM((G, 2 * Z, FP), BF), pltpu.VMEM((Z, 2 * G, FP), BF)
+    wide = pltpu.VMEM((Y, T, FP), BF)
     scratch = [
         pltpu.SemaphoreType.DMA((count,)),
         pltpu.SemaphoreType.DMA((count,)),
+        pltpu.VMEM((6, Y, 1, FP), F32),
         pltpu.VMEM((FP, C * Z * MAIN), BF),
         pltpu.VMEM((X, FP, KR), BF),
         wide, wide, wide, wide,
-        pltpu.VMEM((2, 4, X, C, Z, MAIN, F), BF),
-        pltpu.VMEM((X, C, Z, 8 * R2, F), BF),
-        pltpu.VMEM((8, KR, F), BF),
-        xs, xs, pltpu.VMEM((2, Z, 2 * G, F), BF),
+        pltpu.VMEM((5, X, C, Z, MAIN, FP), BF),
+        pltpu.VMEM((4, X, C, Z, MAIN, FP), BF),
+        pltpu.VMEM((8, KR, FP), BF),
+        pltpu.VMEM((T, FP), BF),
+        xs, xs, pltpu.VMEM((2, Z, 2 * G, FP), BF),
         xs, xs, zs, zs,
-        zs, zs, xs, xs, pltpu.VMEM((T, F), BF),
+        zs, zs, xs, xs, pltpu.VMEM((T, FP), BF),
         zs, zs, xs, xs,
         pltpu.VMEM((T, K), BF),
         pltpu.VMEM((T, KR), BF),
-        pltpu.VMEM((2, 3, T, F), BF),
+        pltpu.VMEM((2, 3, T, FP), BF),
         pltpu.VMEM((2, H * T, T), F32),
-        pltpu.VMEM((T, F), BF),
+        pltpu.VMEM((T, FP), BF),
         pltpu.VMEM((4, T, 1), F32),
-        wide, wide, padded, padded, wide, wide, padded, padded,
-        pltpu.VMEM((2, X, C, Z + 1, MAIN, F), BF),
-        pltpu.VMEM((2, X, Z + 1, MAIN, F), BF),
-        pltpu.VMEM((2, X, Z + 1, MAIN, F), BF),
-        pltpu.VMEM((2, X, Z + 1, MAIN, F), BF),
-        pltpu.VMEM((2, Z, 2, MAIN, F), BF),
-        pltpu.VMEM((2, DP * Z, 2, MAIN, F), BF),
+        wide, wide, wide, wide, wide, wide, wide, wide,
+        pltpu.VMEM((2, X, C, Z + 1, MAIN, FP), BF),
+        pltpu.VMEM((2, X, Z + 1, MAIN, FP), BF),
+        pltpu.VMEM((2, X, Z + 1, MAIN, FP), BF),
+        pltpu.VMEM((2, X, Z + 1, MAIN, FP), BF),
+        pltpu.VMEM((2, Z, MAIN, FP), BF),
+        pltpu.VMEM((2, DP * Z, MAIN, FP), BF),
     ]
     vmem = pl.BlockSpec(memory_space=pltpu.VMEM)
     out, igrad, wg_s, wg_t = pl.pallas_call(
@@ -658,7 +679,7 @@
         compiler_params=pltpu.CompilerParams(
             collective_id=0, has_side_effects=True, vmem_limit_bytes=56 * 2**20
         ),
-    )(tokens.reshape(T, F), cotangent.reshape(T, F), mod, wmain, wrest)
+    )(tokens.reshape(T, F), cotangent.reshape(T, F), modulation[0], wown, wown_t)
     shape = (1, frames, patches, F)
     return out.reshape(shape), igrad.reshape(shape), wg_s, wg_t
 

time: 174 us -> 154 us (0.89); the launches traced: 170 us -> 153 us
  Pallas kernels: 162 us -> 144 us
    pallas_call x1, Pallas kernels: 162 us -> 144 us  [on_device(): pl.pallas_call(functools.partial(kernel, dims, names), out_shape=(jax.Sha...]
    unnamed x20 -> x23, local copies, waits for them, and re-layouts: 5.29 us -> 7.39 us
where the time goes in v2:
time: 154 us; the launch traced here: 153 us
  Pallas kernels  144 us (94%)
  local copies, waits for them, and re-layouts  8.18 us (5%)
    pallas_call x1, Pallas kernels, on_device(): pl.pallas_call(functools.partial(kernel, dims, names), out_shape=(jax.Sha...  144 us
    unnamed x23, local copies, waits for them, and re-layouts  7.39 us

profile of v2, /device:TPU:1, one launch (start us, length us, event | category | flops | bytes accessed | tf_op | source)
XLA Modules:
  0.0 153.2 jit_solution(457395471605620770)
XLA Ops:
  0.6 0.0 copy-start.2
  0.6 1.4 copy.19
  2.0 0.0 copy-done.2
  2.0 0.0 copy-start.6
  2.0 0.7 copy-done.6
  2.8 0.0 copy-start
  2.8 0.0 copy-start.3
  2.8 0.6 copy-done
  3.4 0.2 copy-done.3
  3.6 0.0 copy-start.7
  3.6 0.7 copy-done.7
  4.4 0.0 slice-start
  4.4 0.6 slice.19.wown_t
  5.1 0.1 slice-done
  5.2 0.6 pad_maximum_fusion.wown
  5.8 143.6 %shard_map.102 = (bf16[128,288]{1,0:T(8,128)(2,1)}, bf16[128,288]{1,0:T(8,128)(2,1)}, f32[18,288]{1,0:T(8,128)}, f32[18,288]{1,0:T(8,128)}) custom-call(bf16[128,288]{1,0:T(8,128)(2,1)} %bitcast.20, bf16[128,288]{1,0:T(8,128)(2,1)} %bitcast.21, f32[6,1152]{1,0:T(8,128)} %bitcast.17, bf16[5,16,384]{2,1,0:T(8,128)(2,1)} %pad_maximum_fusion.wown, ...), custom_call_target="tpu_custom_call" | custom-call | tf_op jit(solution)/shard_map/pallas_call | solution.py:668
  149.4 0.0 copy-start.1
  149.4 1.6 %copy.24 = bf16[1,2,64,288]{3,2,1,0:T(8,128)(2,1)} copy(bf16[1,2,64,288]{3,2,1,0:T(8,128)(2,1)} %bitcast.19) | data formatting | bytes 147456
  151.0 0.0 copy-done.1
  151.0 0.0 copy-start.5
  151.0 0.6 copy.25
  151.6 0.1 copy-done.5
  151.8 0.0 copy-start.4
  151.8 0.6 copy.26
  152.4 0.2 copy-done.4
  152.6 0.6 copy.27
  (8 shorter events, 0.1 us)
Async XLA Ops:
  0.6 1.4 copy-start.2
  2.0 0.7 copy-start.6
  2.8 0.6 copy-start
  2.8 0.8 copy-start.3
  3.6 0.7 copy-start.7
  4.4 0.8 slice-start
  149.4 1.6 %copy-start.1 = (bf16[128,288]{1,0:T(8,128)(2,1)S(1)}, bf16[128,288]{1,0:T(8,128)(2,1)}, u32[]{:S(2)}) copy-start(bf16[128,288]{1,0:T(8,128)(2,1)} %get-tuple-element.9) | copy-start | bytes 221188
  151.0 0.8 copy-start.5
  151.8 0.8 copy-start.4

commit v3 on v2

--- a/solution.py
+++ b/solution.py
@@ -167,17 +167,16 @@
         if ndown:
             z_hop(0, 1, b)
 
-    def z_chain(b, arrived):
-        for step in range(nup):
-            z_ = z_take(step, -1, b)
-            if step + 1 < nup:
-                z_hop(step + 1, -1, b)
-            arrived(2 * step + 1, z_)
-            if step < ndown:
-                z_ = z_take(step, 1, b)
-                if step + 1 < ndown:
-                    z_hop(step + 1, 1, b)
-                arrived(2 * step + 2, z_)
+    def z_step(b, step):
+        z_take(step, -1, b)
+        if step + 1 < nup:
+            z_hop(step + 1, -1, b)
+        if step >= ndown:
+            return [2 * step + 1]
+        z_take(step, 1, b)
+        if step + 1 < ndown:
+            z_hop(step + 1, 1, b)
+        return [2 * step + 1, 2 * step + 2]
 
     def order(i):
         return lax.rem(z + (-(i + 1) // 2 if i % 2 else i // 2) + Z, Z)
@@ -459,14 +458,14 @@
         for n in range(F // WP):
             ref[MAIN : MAIN + R2, n * WP : (n + 1) * WP] = tail[n * R2 : (n + 1) * R2, 128 - WP :]
 
-    late = 2
-
-    def arrived(i, z_):
-        x_hop(i)
-        if i >= late:
-            x_take(i - late)
-
-    z_chain(0, arrived)
+    before = [0]
+    for step in range(nup):
+        here = z_step(0, step)
+        for i in here:
+            x_hop(i)
+        for i in before:
+            x_take(i)
+        before = here
     z_start(1)
 
     ex_wait(cot_b, names["cot_x"], G, g)
@@ -477,9 +476,8 @@
     ex_wait(xw_s, names["tok"], Y, y)
     norm(xw_s, 0)
 
-    for i in range(Z - late, Z):
+    for i in before:
         x_take(i)
-    z_chain(1, lambda i, z_: None)
     if X > 2:
         for i in range(Z):
             x_last(i)
@@ -493,10 +491,15 @@
     def to_sibling(x_, n):
         send(Wt.at[:, x_, c], Wt.at[:, x_, c], names["sib1"] + n, sibling)
 
-    for k in range(1, X):
-        to_x = lax.rem(x + k, X)
-        send(Wt.at[:, x, c], Wt.at[:, x, c], names["xp1"] + k, dev_x(to_x))
-    to_sibling(x, 0)
+    z_steps = iter(range(nup))
+
+    def z_later(n):
+        for _ in range(n):
+            step = next(z_steps, None)
+            if step is not None:
+                z_step(1, step)
+
+    z_later(1)
 
     ex_wait(cot_c.at[1], names["cot_z"], Z, z)
     cot_t = flatten(cot_c.at[1])
@@ -512,30 +515,35 @@
         Wr[:, x_ * CZ * R2 : (x_ + 1) * CZ * R2] = rest.reshape(8, CZ * R2, FP)
 
     project(0)
+    z_later(1)
     flat_s[...] = attend(0)
+    z_later(1)
     out_partial(0, flat_s[...], rs1_a)
     ex_send(lambda p: rs1_a.at[p], rs1_b, names["rs1"], Y, y, dev_y)
     rs1_b[y] = rs1_a[y]
 
+    z_later(nup)
     for k in range(1, X):
-        x_ = lax.rem(x + X - k, X)
-        recv(Wt.at[:, x_, c], names["xp1"] + k)
-        to_sibling(x_, k)
-
+        to_x = lax.rem(x + k, X)
+        send(Wt.at[:, x, c], Wt.at[:, x, c], names["xp1"] + k, dev_x(to_x))
+    to_sibling(x, 0)
     ex_wait(rs1_b, names["rs1"], Y, y)
     first = xw_s[y].astype(F32) + mod[2, y] * add_up(rs1_b)
     x_put(fst_a, to_groups(first.astype(BF)))
     ex_send(lambda p: fst_a.at[p], fst_b, names["fst_x"], G, g, dev_g)
     fst_b[g] = fst_a[g]
-
-    for k in range(X):
-        recv(Wt.at[:, lax.rem(x + X - k, X), 1 - c], names["sib1"] + k)
-    ex_wait(gw_t, names["ggt"], Y, y)
-
     ex_wait(fst_b, names["fst_x"], G, g)
     z_put(fst_c, to_z(flatten(fst_b)))
     ex_send(lambda p: fst_c.at[p], fst_d, names["fst_z"], Z, z, dev_z)
     fst_d[z] = fst_c[z]
+    for k in range(1, X):
+        x_ = lax.rem(x + X - k, X)
+        recv(Wt.at[:, x_, c], names["xp1"] + k)
+        to_sibling(x_, k)
+
+    for k in range(X):
+        recv(Wt.at[:, lax.rem(x + X - k, X), 1 - c], names["sib1"] + k)
+    ex_wait(gw_t, names["ggt"], Y, y)
 
     ex_wait(fst_d, names["fst_z"], Z, z)
     xw_t[y] = flatten(fst_d)
@@ -607,6 +615,11 @@
     wg_end(0, wg_s)
     for copy in sent:
         copy.wait_send()
+
+
+def hand_on(*refs):
+    for source, target in zip(refs[:4], refs[4:]):
+        target[...] = source[...]
 
 
 def on_device(sizes, tokens, modulation, qkv_s, out_s, qkv_t, out_t, cotangent):
@@ -680,6 +693,12 @@
             collective_id=0, has_side_effects=True, vmem_limit_bytes=56 * 2**20
         ),
     )(tokens.reshape(T, F), cotangent.reshape(T, F), modulation[0], wown, wown_t)
+    out, igrad, wg_s, wg_t = pl.pallas_call(
+        hand_on,
+        out_shape=tuple(jax.ShapeDtypeStruct(v.shape, v.dtype) for v in (out, igrad, wg_s, wg_t)),
+        in_specs=[vmem] * 4,
+        out_specs=(vmem,) * 4,
+    )(out, igrad, wg_s, wg_t)
     shape = (1, frames, patches, F)
     return out.reshape(shape), igrad.reshape(shape), wg_s, wg_t
 

time: 154 us -> 149 us (0.968)
  local copies, waits for them, and re-layouts: 8.18 us -> 4.43 us
  Pallas kernels: 144 us -> 142 us
    unnamed x23 -> x13, local copies, waits for them, and re-layouts: 7.39 us -> 3.65 us
    pallas_call x1, Pallas kernels: 144 us -> 141 us  [on_device(): pl.pallas_call(functools.partial(kernel, dims, names), out_shape=(jax.Sha...]
    pallas_call x0 -> x1, Pallas kernels: none -> 1.65 us  [on_device(): pl.pallas_call(hand_on, out_shape=tuple((jax.ShapeDtypeStruct(v.shape, v....]
where the time goes in v3:
time: 149 us; the launch traced here: 148 us
  Pallas kernels  142 us (95%)
  local copies, waits for them, and re-layouts  4.43 us (3%)
    pallas_call x1, Pallas kernels, on_device(): pl.pallas_call(functools.partial(kernel, dims, names), out_shape=(jax.Sha...  141 us
    unnamed x13, local copies, waits for them, and re-layouts  3.65 us

profile of v3, /device:TPU:1, one launch (start us, length us, event | category | flops | bytes accessed | tf_op | source)
XLA Modules:
  0.0 148.3 jit_solution(1144941558699411129)
XLA Ops:
  0.6 0.0 copy-start.1
  0.6 1.4 copy.19
  2.0 0.0 copy-done.1
  2.0 0.0 copy-start.3
  2.0 0.7 copy-done.3
  2.8 0.0 copy-start
  2.8 0.0 copy-start.2
  2.8 0.6 copy-done
  3.4 0.2 copy-done.2
  3.6 0.0 copy-start.4
  3.6 0.7 copy-done.4
  4.4 0.0 slice-start
  4.4 0.6 slice.19.wown_t
  5.1 0.1 slice-done
  5.2 0.6 pad_maximum_fusion.wown
  5.8 140.8 %shard_map.102 = (bf16[128,288]{1,0:T(8,128)(2,1)}, bf16[128,288]{1,0:T(8,128)(2,1)}, f32[18,288]{1,0:T(8,128)}, f32[18,288]{1,0:T(8,128)}) custom-call(bf16[128,288]{1,0:T(8,128)(2,1)} %bitcast.18, bf16[128,288]{1,0:T(8,128)(2,1)} %bitcast.19, f32[6,1152]{1,0:T(8,128)} %bitcast.17, bf16[5,16,384]{2,1,0:T(8,128)(2,1)} %pad_maximum_fusion.wown, ...), custom_call_target="tpu_custom_call" | custom-call | tf_op jit(solution)/shard_map/pallas_call | solution.py:681
  146.6 1.7 %shard_map.103 = (bf16[128,288]{1,0:T(8,128)(2,1)}, bf16[128,288]{1,0:T(8,128)(2,1)}, f32[18,288]{1,0:T(8,128)}, f32[18,288]{1,0:T(8,128)}) custom-call(bf16[128,288]{1,0:T(8,128)(2,1)} %get-tuple-element.12.refs_0_, bf16[128,288]{1,0:T(8,128)(2,1)} %get-tuple-element.13.refs_1_, f32[18,288]{1,0:T(8,128)} %get-tuple-element.14.refs_2_, ...), custom_call_target="tpu_custom_call" | custom-call | tf_op jit(solution)/shard_map/pallas_call | solution.py:696
  (8 shorter events, 0.1 us)
Async XLA Ops:
  0.6 1.4 copy-start.1
  2.0 0.7 copy-start.3
  2.8 0.6 copy-start
  2.8 0.8 copy-start.2
  3.6 0.7 copy-start.4
  4.4 0.8 slice-start

commit v4 on v3

--- a/solution.py
+++ b/solution.py
@@ -63,12 +63,12 @@
     return names, s.count
 
 
-def kernel(dims, names, tok, cot, mods, wown, wown_t, out, igrad, wg_s, wg_t, *refs):
+def kernel(dims, names, tok, cot, mods, qkv_s, out_s, qkv_t, out_t, out, igrad, wg_s, wg_t, *refs):
     X, C, Z, Y, DP, T, F, FP, H, R2 = dims
     G = X * C
     N = Y * F
     (
-        ssem, rsem, mod, pm, pr, xw_s, xw_t, gw_t, gw_s, Ws, Wt, Wr, cotp,
+        ssem, rsem, wown, wown_t, mod, pm, pr, xw_s, xw_t, gw_t, gw_s, Ws, Wt, Wr, cotp,
         cot_a, cot_b, cot_c, fst_a, fst_b, fst_c, fst_d, fg_a, fg_b, fg_c, fg_d, fg_e,
         out_a, out_b, out_c, out_d,
         mp, mpr, qkv, prob, flat_s, stat,
@@ -139,6 +139,22 @@
     peers += [dev_zg(lax.rem(zg + k, ZG)) for k in range(1, ZG)]
     for peer in peers:
         pl.semaphore_signal(barrier, inc=1, device_id=peer, device_id_type=MESH)
+
+    rows = MAIN + R2
+
+    def widened(value):
+        return jnp.concatenate([value, jnp.zeros((value.shape[0], FP - F), F32)], axis=1)
+
+    rest = []
+    for ref, qkv_ref, out_ref in ((wown, qkv_s, out_s), (wown_t, qkv_t, out_t)):
+        value = qkv_ref[...].astype(F32)
+        for k in range(4):
+            part = value[:, k, :] if k < 3 else out_ref[...].astype(F32)
+            part = widened(part.reshape(rows, F))
+            ref[k] = part[:MAIN].astype(BF)
+            rest.append(part[MAIN:])
+    wown[4] = jnp.concatenate(rest, axis=0).astype(BF)
+
     pl.semaphore_wait(barrier, len(peers))
 
     up, down = dev_zg(lax.rem(zg + 1, ZG)), dev_zg(lax.rem(zg + ZG - 1, ZG))
@@ -257,7 +273,7 @@
     mod[...] = jnp.zeros((6, Y, 1, FP), F32)
     for i in range(6):
         for n in range(Y):
-            mod[i, n, :, :F] = mods[i : i + 1, n * F : (n + 1) * F]
+            mod[i, n, :, :F] = mods[0, i : i + 1, n * F : (n + 1) * F]
 
     CZ = C * Z
     j = iota((FP, CZ * MAIN), 1)
@@ -636,21 +652,14 @@
     dims = (X, C, Z, Y, DP, T, F, FP, H, R2)
     names, count = layout(X, C, Z, Y, DP)
 
-    def joined(qkv, out):
-        both = jnp.concatenate([qkv.transpose(1, 0, 2), out[None]], axis=0)
-        return jnp.pad(both, ((0, 0), (0, 0), (0, FP - F)))
-
-    first, second = joined(qkv_s, out_s), joined(qkv_t, out_t)
-    rest = jnp.concatenate([first[:, MAIN:], second[:, MAIN:]]).reshape(1, 8 * R2, FP)
-    wown = jnp.concatenate([first[:, :MAIN], rest])
-    wown_t = second[:, :MAIN]
-
     K, KR = X * C * Z * MAIN, X * C * Z * R2
     xs, zs = pltpu.VMEM((G, 2 * Z, FP), BF), pltpu.VMEM((Z, 2 * G, FP), BF)
     wide = pltpu.VMEM((Y, T, FP), BF)
     scratch = [
         pltpu.SemaphoreType.DMA((count,)),
         pltpu.SemaphoreType.DMA((count,)),
+        pltpu.VMEM((5, MAIN, FP), BF),
+        pltpu.VMEM((4, MAIN, FP), BF),
         pltpu.VMEM((6, Y, 1, FP), F32),
         pltpu.VMEM((FP, C * Z * MAIN), BF),
         pltpu.VMEM((X, FP, KR), BF),
@@ -686,13 +695,13 @@
             jax.ShapeDtypeStruct((rows, F), F32),
             jax.ShapeDtypeStruct((rows, F), F32),
         ),
-        in_specs=[vmem] * 5,
+        in_specs=[vmem] * 7,
         out_specs=(vmem,) * 4,
         scratch_shapes=scratch,
         compiler_params=pltpu.CompilerParams(
             collective_id=0, has_side_effects=True, vmem_limit_bytes=56 * 2**20
         ),
-    )(tokens.reshape(T, F), cotangent.reshape(T, F), modulation[0], wown, wown_t)
+    )(tokens.reshape(T, F), cotangent.reshape(T, F), modulation, qkv_s, out_s, qkv_t, out_t)
     out, igrad, wg_s, wg_t = pl.pallas_call(
         hand_on,
         out_shape=tuple(jax.ShapeDtypeStruct(v.shape, v.dtype) for v in (out, igrad, wg_s, wg_t)),

time: 149 us -> 145 us (0.973)
  local copies, waits for them, and re-layouts: 4.43 us -> 1.37 us
    unnamed x13 -> x1, local copies, waits for them, and re-layouts: 3.65 us -> 1.37 us
where the time goes in v4:
time: 145 us; the launch traced here: 144 us
  Pallas kernels  142 us (98%)
    pallas_call x1, Pallas kernels, on_device(): pl.pallas_call(functools.partial(kernel, dims, names), out_shape=(jax.Sha...  141 us

profile of v4, /device:TPU:1, one launch (start us, length us, event | category | flops | bytes accessed | tf_op | source)
XLA Modules:
  0.0 144.2 jit_solution(11592917955894349412)
XLA Ops:
  0.6 1.4 copy.11.mods
  2.0 140.5 %shard_map.102 = (bf16[128,288]{1,0:T(8,128)(2,1)}, bf16[128,288]{1,0:T(8,128)(2,1)}, f32[18,288]{1,0:T(8,128)}, f32[18,288]{1,0:T(8,128)}) custom-call(bf16[128,288]{1,0:T(8,128)(2,1)} %bitcast.4, bf16[128,288]{1,0:T(8,128)(2,1)} %bitcast.5, f32[1,6,1152]{2,1,0:T(8,128)} %copy.11.mods, bf16[18,3,288]{2,1,0:T(4,128)(2,1)} %qkv_s.1, bf16[18,288]{1,0:T(8,128)(2,1)} %out_s.1, ...), custom_call_target="tpu_custom_call" | custom-call | tf_op jit(solution)/shard_map/pallas_call | solution.py:690
  142.5 1.7 %shard_map.103 = (bf16[128,288]{1,0:T(8,128)(2,1)}, bf16[128,288]{1,0:T(8,128)(2,1)}, f32[18,288]{1,0:T(8,128)}, f32[18,288]{1,0:T(8,128)}) custom-call(bf16[128,288]{1,0:T(8,128)(2,1)} %get-tuple-element.12.refs_0_, bf16[128,288]{1,0:T(8,128)(2,1)} %get-tuple-element.13.refs_1_, f32[18,288]{1,0:T(8,128)} %get-tuple-element.14.refs_2_, ...), custom_call_target="tpu_custom_call" | custom-call | tf_op jit(solution)/shard_map/pallas_call | solution.py:705

commit v5 on v4

--- a/solution.py
+++ b/solution.py
@@ -45,7 +45,7 @@
     s = Sems()
     names = {}
     G = X * C
-    for name in ("tok", "ggt", "rs1", "fst", "rsg", "rsp", "ggs", "rsf"):
+    for name in ("tok", "ggt", "rs1", "fst", "rsg", "rsp", "ggs", "rsf", "hw"):
         names[name] = s.take(Y)
     for name in ("cot_x", "fst_x", "fg_x", "out_x"):
         names[name] = s.take(G)
@@ -71,7 +71,7 @@
         ssem, rsem, wown, wown_t, mod, pm, pr, xw_s, xw_t, gw_t, gw_s, Ws, Wt, Wr, cotp,
         cot_a, cot_b, cot_c, fst_a, fst_b, fst_c, fst_d, fg_a, fg_b, fg_c, fg_d, fg_e,
         out_a, out_b, out_c, out_d,
-        mp, mpr, qkv, prob, flat_s, stat,
+        mp, mpr, qkv, prob, flat_s, hw, stat,
         rs1_a, rs1_b, rsg_a, rsg_b, rsp_a, rsp_b, rsf_a, rsf_b,
         wgp, wgc, wgx, wgxr, wgz, wgzr,
     ) = refs
@@ -139,6 +139,14 @@
     peers += [dev_zg(lax.rem(zg + k, ZG)) for k in range(1, ZG)]
     for peer in peers:
         pl.semaphore_signal(barrier, inc=1, device_id=peer, device_id_type=MESH)
+    aligned = x == y
+    corner = [(dev(d, y, z, c, n), aligned & (y == n)) for n in range(Y)]
+    corner += [(dev(d, n, z, c, x), aligned & (x == n)) for n in range(X)]
+    for peer, own in corner:
+
+        @pl.when(jnp.logical_not(own))
+        def _(peer=peer):
+            pl.semaphore_signal(barrier, inc=1, device_id=peer, device_id_type=MESH)
 
     rows = MAIN + R2
 
@@ -155,7 +163,7 @@
             rest.append(part[MAIN:])
     wown[4] = jnp.concatenate(rest, axis=0).astype(BF)
 
-    pl.semaphore_wait(barrier, len(peers))
+    pl.semaphore_wait(barrier, len(peers) + jnp.where(aligned, len(corner) - 2, len(corner)))
 
     up, down = dev_zg(lax.rem(zg + 1, ZG)), dev_zg(lax.rem(zg + ZG - 1, ZG))
     right, left = lax.rem(x + 1, X), lax.rem(x + X - 1, X)
@@ -441,8 +449,49 @@
         ex_send(lambda p: wgx.at[b, p], wgxr.at[b], names["wx%d" % b], X, x, dev_x)
         wgxr[b, x] = wgx[b, x]
 
+    def wg_start_own(grad):
+        main = mm(grad, pm[...]).astype(BF)
+        rest = mm(grad, pr[0]).astype(BF)
+        for n in range(Y):
+            wgp[0, n, :, :Z] = mm_tn(main, hw[n]).astype(BF).reshape(C, Z, MAIN, FP)
+            part = mm_tn(rest, hw[n])[: CZ * R2].astype(BF)
+            wgp[0, n, :, Z] = part.reshape(C, Z * R2, FP)
+        send(wgp.at[0, :, 1 - c], wgc.at[0], names["wc0"], sibling)
+
+    corner_sent = []
+
+    def wg_second_own():
+        recv(wgc.at[0], names["wc0"])
+        wgx[0] = (wgp[0, :, c].astype(F32) + wgc[0].astype(F32)).astype(BF)
+        for n in range(Y):
+            peer, own = corner[n]
+            copy = pltpu.make_async_remote_copy(
+                src_ref=wgx.at[0, n], dst_ref=wgxr.at[0, x],
+                send_sem=ssem.at[names["wx0"] + n], recv_sem=rsem.at[names["wx0"] + x],
+                device_id=peer, device_id_type=MESH,
+            )
+            corner_sent.append((copy, own))
+
+            @pl.when(jnp.logical_not(own))
+            def _(copy=copy):
+                copy.start()
+
+            @pl.when(own)
+            def _(n=n):
+                wgxr[0, x] = wgx[0, n]
+
+    def wg_wait_own():
+        for n in range(X):
+
+            @pl.when(jnp.logical_not(corner[Y + n][1]))
+            def _(n=n):
+                recv(wgxr.at[0, n], names["wx0"] + n)
+
     def wg_third(b):
-        ex_wait(wgxr.at[b], names["wx%d" % b], X, x)
+        if b == 0:
+            wg_wait_own()
+        else:
+            ex_wait(wgxr.at[b], names["wx%d" % b], X, x)
         total = wgxr[b, 0].astype(F32)
         for n in range(1, X):
             total = total + wgxr[b, n].astype(F32)
@@ -569,6 +618,8 @@
     grad_t = grad_heads(1)
 
     ex_wait(xw_t, names["fst"], Y, y)
+    hw[y] = flat_s[...]
+    ex_send(lambda p: hw.at[y], hw, names["hw"], Y, y, dev_y)
     norm(xw_t, 1)
     project(1)
     flat_t = attend(1)
@@ -593,6 +644,7 @@
     x_put(fg_c, from_z(flatten(fg_b)))
     ex_send(lambda p: fg_c.at[p], fg_d, names["fg_x"], G, g, dev_g)
     fg_d[g] = fg_c[g]
+    wg_second(1)
 
     ex_wait(rsp_b, names["rsp"], Y, y)
     second = xw_t[y].astype(F32) + mod[5, y] * add_up(rsp_b)
@@ -605,18 +657,18 @@
     gw_s[y] = gated(0, fg_e[...])
     ex_send(lambda p: gw_s.at[y], gw_s, names["ggs"], Y, y, dev_y)
 
-    wg_second(1)
+    ex_wait(hw, names["hw"], Y, y)
+    wg_start_own(gw_s[y])
     ex_wait(out_b, names["out_z"], Z, z)
     x_put(out_c, from_z(flatten(out_b)))
     ex_send(lambda p: out_c.at[p], out_d, names["out_x"], G, g, dev_g)
     out_d[g] = out_c[g]
+    wg_second_own()
 
     ex_wait(gw_s, names["ggs"], Y, y)
     narrow([gw_s[n] for n in range(Y)])
-    wg_start(0, flat_s[...])
+    wg_third(1)
     grad_s = grad_heads(0)
-    wg_third(1)
-    wg_second(0)
     grads = attend_back(0, grad_s)
     wg_third(0)
     in_partial(0, grads, xw_s, rsf_a)
@@ -631,6 +683,11 @@
     wg_end(0, wg_s)
     for copy in sent:
         copy.wait_send()
+    for copy, own in corner_sent:
+
+        @pl.when(jnp.logical_not(own))
+        def _(copy=copy):
+            copy.wait_send()
 
 
 def hand_on(*refs):
@@ -677,6 +734,7 @@
         pltpu.VMEM((2, 3, T, FP), BF),
         pltpu.VMEM((2, H * T, T), F32),
         pltpu.VMEM((T, FP), BF),
+        wide,
         pltpu.VMEM((4, T, 1), F32),
         wide, wide, wide, wide, wide, wide, wide, wide,
         pltpu.VMEM((2, X, C, Z + 1, MAIN, FP), BF),

time: 145 us -> 155 us (1.069)
  the two profiles are of different devices: /device:TPU:1 before, /device:TPU:4 now
where the time goes in v5:
time: 155 us
  Pallas kernels  153 us (99%)
    pallas_call x1, Pallas kernels, on_device(): pl.pallas_call(functools.partial(kernel, dims, names), out_shape=(jax.Sha...  151 us

profile of v5, /device:TPU:4, one launch (start us, length us, event | category | flops | bytes accessed | tf_op | source)
XLA Modules:
  0.0 155.1 jit_solution(13651755251065032202)
XLA Ops:
  0.6 1.4 copy.11.mods
  2.0 151.5 %shard_map.102 = (bf16[128,288]{1,0:T(8,128)(2,1)}, bf16[128,288]{1,0:T(8,128)(2,1)}, f32[18,288]{1,0:T(8,128)}, f32[18,288]{1,0:T(8,128)}) custom-call(bf16[128,288]{1,0:T(8,128)(2,1)} %bitcast.4, bf16[128,288]{1,0:T(8,128)(2,1)} %bitcast.5, f32[1,6,1152]{2,1,0:T(8,128)} %copy.11.mods, bf16[18,3,288]{2,1,0:T(4,128)(2,1)} %qkv_s.1, bf16[18,288]{1,0:T(8,128)(2,1)} %out_s.1, ...), custom_call_target="tpu_custom_call" | custom-call | tf_op jit(solution)/shard_map/pallas_call | solution.py:748
  153.5 1.7 %shard_map.103 = (bf16[128,288]{1,0:T(8,128)(2,1)}, bf16[128,288]{1,0:T(8,128)(2,1)}, f32[18,288]{1,0:T(8,128)}, f32[18,288]{1,0:T(8,128)}) custom-call(bf16[128,288]{1,0:T(8,128)(2,1)} %get-tuple-element.12.refs_0_, bf16[128,288]{1,0:T(8,128)(2,1)} %get-tuple-element.13.refs_1_, f32[18,288]{1,0:T(8,128)} %get-tuple-element.14.refs_2_, ...), custom_call_target="tpu_custom_call" | custom-call | tf_op jit(solution)/shard_map/pallas_call | solution.py:763

commit v6 on v4

--- a/solution.py
+++ b/solution.py
@@ -59,6 +59,8 @@
     for b in (0, 1):
         names["wc%d" % b] = s.take(1)
         names["wx%d" % b] = s.take(X)
+        names["wy%d" % b] = s.take(X)
+        names["wr%d" % b] = s.take(X)
         names["wz%d" % b] = s.take(DP * Z)
     return names, s.count
 
@@ -117,6 +119,10 @@
         )
         copy.start()
         sent.append(copy)
+
+    def drain(keep=0):
+        while len(sent) > keep:
+            sent.pop(0).wait_send()
 
     def recv(dst, sem):
         pltpu.make_async_remote_copy(
@@ -273,7 +279,7 @@
     mod[...] = jnp.zeros((6, Y, 1, FP), F32)
     for i in range(6):
         for n in range(Y):
-            mod[i, n, :, :F] = mods[0, i : i + 1, n * F : (n + 1) * F]
+            mod[i, n, :, :F] = mods[i, :, n * F : (n + 1) * F]
 
     CZ = C * Z
     j = iota((FP, CZ * MAIN), 1)
@@ -421,6 +427,9 @@
     def gated(b, value):
         return (mod[3 * b + 2, y] * value.astype(F32)).astype(BF)
 
+    HZ = Z // 2
+    near = z // HZ * HZ
+    far = HZ - near
     FULL = FP - 128
     WP = 128 - (F - FULL)
 
@@ -438,30 +447,47 @@
     def wg_second(b):
         recv(wgc.at[b], names["wc%d" % b])
         wgx[b] = (wgp[b, :, c].astype(F32) + wgc[b].astype(F32)).astype(BF)
-        ex_send(lambda p: wgx.at[b, p], wgxr.at[b], names["wx%d" % b], X, x, dev_x)
+        for name, start in (("wx%d" % b, far), ("wr%d" % b, Z), ("wy%d" % b, near)):
+            blocks = pl.ds(start, 1 if name[1] == "r" else HZ)
+            for k in range(1, X):
+                to_x = lax.rem(x + k, X)
+                send(wgx.at[b, to_x, blocks], wgxr.at[b, x, blocks], names[name] + k, dev_x(to_x))
         wgxr[b, x] = wgx[b, x]
 
-    def wg_third(b):
-        ex_wait(wgxr.at[b], names["wx%d" % b], X, x)
-        total = wgxr[b, 0].astype(F32)
+    def wg_take(b, name, blocks):
+        for k in range(1, X):
+            recv(wgxr.at[b, lax.rem(x + X - k, X), blocks], names[name + str(b)] + k)
+        total = wgxr[b, 0, blocks].astype(F32)
         for n in range(1, X):
-            total = total + wgxr[b, n].astype(F32)
-        total = total.astype(BF)
-        main, rest = total[:Z].reshape(Z * MAIN, FP), total[Z]
-        wgz[b, :, :, :FULL] = main[:, :FULL].reshape(Z, MAIN, FULL)
+            total = total + wgxr[b, n, blocks].astype(F32)
+        return total.astype(BF)
+
+    def wg_third(b, start):
+        blocks = pl.ds(start, HZ)
+        main = wg_take(b, "wx" if start is far else "wy", blocks).reshape(HZ * MAIN, FP)
+        if start is far:
+            wgxr[b, 0, Z] = wg_take(b, "wr", pl.ds(Z, 1))[0]
+        rest = wgxr[b, 0, Z]
+        wgz[b, blocks, :, :FULL] = main[:, :FULL].reshape(HZ, MAIN, FULL)
         tail = main[:, FULL:].astype(F32)
         for n in range(F // WP):
             pick = shift_lanes(n)
-            o = iota((Z * MAIN, Z * R2), 0)
+            o = iota((HZ * MAIN, Z * R2), 0)
             slot = lax.rem(o, MAIN) - n * R2
-            rows = (o // MAIN) * R2 + slot == iota((Z * MAIN, Z * R2), 1)
+            rows = (o // MAIN + start) * R2 + slot == iota((HZ * MAIN, Z * R2), 1)
             rows = (rows & (slot >= 0) & (slot < R2)).astype(BF)
             tail = tail + mm(rows, mm(rest, pick).astype(BF))
-        wgz[b, :, :, FULL:] = tail.astype(BF).reshape(Z, MAIN, 128)
-        ex_send(
-            lambda p: wgz.at[b, lax.rem(p, Z)], wgzr.at[b], names["wz%d" % b], ZG, zg, dev_zg
-        )
-        wgzr[b, zg] = wgz[b, z]
+        wgz[b, blocks, :, FULL:] = tail.astype(BF).reshape(HZ, MAIN, 128)
+        for m in range(HZ):
+            for e in range(DP):
+                if start is near and m == 0 and e == 0:
+                    continue
+                z_ = start + lax.rem(lax.rem(z, HZ) + m, HZ)
+                peer = lax.rem(d + e, DP) * Z + z_
+                hop = lax.rem(peer + ZG - zg, ZG)
+                send(wgz.at[b, z_], wgzr.at[b, zg], names["wz%d" % b] + hop, dev_zg(peer))
+        if start is near:
+            wgzr[b, zg] = wgz[b, z]
 
     def wg_end(b, ref):
         ex_wait(wgzr.at[b], names["wz%d" % b], ZG, zg)
@@ -543,6 +569,7 @@
         to_x = lax.rem(x + k, X)
         send(Wt.at[:, x, c], Wt.at[:, x, c], names["xp1"] + k, dev_x(to_x))
     to_sibling(x, 0)
+    drain(20)
     ex_wait(rs1_b, names["rs1"], Y, y)
     first = xw_s[y].astype(F32) + mod[2, y] * add_up(rs1_b)
     x_put(fst_a, to_groups(first.astype(BF)))
@@ -567,6 +594,7 @@
 
     narrow([gw_t[n] for n in range(Y)])
     grad_t = grad_heads(1)
+    drain(2 * Y)
 
     ex_wait(xw_t, names["fst"], Y, y)
     norm(xw_t, 1)
@@ -593,6 +621,7 @@
     x_put(fg_c, from_z(flatten(fg_b)))
     ex_send(lambda p: fg_c.at[p], fg_d, names["fg_x"], G, g, dev_g)
     fg_d[g] = fg_c[g]
+    wg_second(1)
 
     ex_wait(rsp_b, names["rsp"], Y, y)
     second = xw_t[y].astype(F32) + mod[5, y] * add_up(rsp_b)
@@ -605,32 +634,35 @@
     gw_s[y] = gated(0, fg_e[...])
     ex_send(lambda p: gw_s.at[y], gw_s, names["ggs"], Y, y, dev_y)
 
-    wg_second(1)
     ex_wait(out_b, names["out_z"], Z, z)
     x_put(out_c, from_z(flatten(out_b)))
     ex_send(lambda p: out_c.at[p], out_d, names["out_x"], G, g, dev_g)
     out_d[g] = out_c[g]
 
+    drain(Y + G)
+
     ex_wait(gw_s, names["ggs"], Y, y)
     narrow([gw_s[n] for n in range(Y)])
     wg_start(0, flat_s[...])
     grad_s = grad_heads(0)
-    wg_third(1)
+    wg_third(1, far)
     wg_second(0)
+    wg_third(1, near)
     grads = attend_back(0, grad_s)
-    wg_third(0)
+    wg_third(0, far)
     in_partial(0, grads, xw_s, rsf_a)
     ex_send(lambda p: rsf_a.at[p], rsf_b, names["rsf"], Y, y, dev_y)
     rsf_b[y] = rsf_a[y]
+    wg_third(0, near)
 
     ex_wait(out_d, names["out_x"], G, g)
     out[...] = from_groups(flatten(out_d))[:, :F]
     wg_end(1, wg_t)
     ex_wait(rsf_b, names["rsf"], Y, y)
     igrad[...] = in_finish(0, rsf_b, xw_s, fg_e[...])[:, :F]
+    drain()
     wg_end(0, wg_s)
-    for copy in sent:
-        copy.wait_send()
+    drain()
 
 
 def hand_on(*refs):
@@ -701,7 +733,7 @@
         compiler_params=pltpu.CompilerParams(
             collective_id=0, has_side_effects=True, vmem_limit_bytes=56 * 2**20
         ),
-    )(tokens.reshape(T, F), cotangent.reshape(T, F), modulation, qkv_s, out_s, qkv_t, out_t)
+    )(tokens.reshape(T, F), cotangent.reshape(T, F), modulation.transpose(1, 0, 2), qkv_s, out_s, qkv_t, out_t)
     out, igrad, wg_s, wg_t = pl.pallas_call(
         hand_on,
         out_shape=tuple(jax.ShapeDtypeStruct(v.shape, v.dtype) for v in (out, igrad, wg_s, wg_t)),

time: 145 us -> 143 us (0.986)
  no operation moved by 1% of the time
where the time goes in v6:
time: 143 us; the launch traced here: 142 us
  Pallas kernels  141 us (99%)
    pallas_call x1, Pallas kernels, on_device(): pl.pallas_call(functools.partial(kernel, dims, names), out_shape=(jax.Sha...  139 us

profile of v6, /device:TPU:1, one launch (start us, length us, event | category | flops | bytes accessed | tf_op | source)
XLA Modules:
  0.0 141.6 jit_solution(3080993660798370985)
XLA Ops:
  0.6 139.3 %shard_map.102 = (bf16[128,288]{1,0:T(8,128)(2,1)}, bf16[128,288]{1,0:T(8,128)(2,1)}, f32[18,288]{1,0:T(8,128)}, f32[18,288]{1,0:T(8,128)}) custom-call(bf16[128,288]{1,0:T(8,128)(2,1)} %bitcast.5, bf16[128,288]{1,0:T(8,128)(2,1)} %bitcast.6, f32[6,1,1152]{2,1,0:T(1,128)} %bitcast.7, bf16[18,3,288]{2,1,0:T(4,128)(2,1)} %qkv_s.1, bf16[18,288]{1,0:T(8,128)(2,1)} %out_s.1, ...), custom_call_target="tpu_custom_call" | custom-call | tf_op jit(solution)/shard_map/pallas_call | solution.py:722
  139.9 1.7 %shard_map.103 = (bf16[128,288]{1,0:T(8,128)(2,1)}, bf16[128,288]{1,0:T(8,128)(2,1)}, f32[18,288]{1,0:T(8,128)}, f32[18,288]{1,0:T(8,128)}) custom-call(bf16[128,288]{1,0:T(8,128)(2,1)} %get-tuple-element.12.refs_0_, bf16[128,288]{1,0:T(8,128)(2,1)} %get-tuple-element.13.refs_1_, f32[18,288]{1,0:T(8,128)} %get-tuple-element.14.refs_2_, ...), custom_call_target="tpu_custom_call" | custom-call | tf_op jit(solution)/shard_map/pallas_call | solution.py:737

commit v7 on v6

--- a/solution.py
+++ b/solution.py
@@ -54,7 +54,7 @@
     for name in ("zu0", "zd0", "zu1", "zd1", "xr0", "xl0", "xo0"):
         names[name] = s.take(Z)
     names["sib0"] = s.take(X * Z)
-    names["xp1"] = s.take(X)
+    names["xp1"] = s.take(X * Z)
     names["sib1"] = s.take(X)
     for b in (0, 1):
         names["wc%d" % b] = s.take(1)
@@ -539,7 +539,10 @@
         for _ in range(n):
             step = next(z_steps, None)
             if step is not None:
-                z_step(1, step)
+                for i in z_step(1, step) + ([0] if step == 0 else []):
+                    slot = w_slot(1, x, c, order(i))
+                    for k in range(1, X):
+                        send(slot, slot, names["xp1"] + k * Z + i, dev_x(lax.rem(x + k, X)))
 
     z_later(1)
 
@@ -565,9 +568,6 @@
     rs1_b[y] = rs1_a[y]
 
     z_later(nup)
-    for k in range(1, X):
-        to_x = lax.rem(x + k, X)
-        send(Wt.at[:, x, c], Wt.at[:, x, c], names["xp1"] + k, dev_x(to_x))
     to_sibling(x, 0)
     drain(20)
     ex_wait(rs1_b, names["rs1"], Y, y)
@@ -581,7 +581,8 @@
     fst_d[z] = fst_c[z]
     for k in range(1, X):
         x_ = lax.rem(x + X - k, X)
-        recv(Wt.at[:, x_, c], names["xp1"] + k)
+        for i in range(Z):
+            recv(w_slot(1, x_, c, order(i)), names["xp1"] + k * Z + i)
         to_sibling(x_, k)
 
     for k in range(X):

time: 143 us -> 136 us (0.951)
  Pallas kernels: 141 us -> 135 us
    pallas_call x1, Pallas kernels: 139 us -> 134 us  [on_device(): pl.pallas_call(functools.partial(kernel, dims, names), out_shape=(jax.Sha...]
where the time goes in v7:
time: 136 us
  Pallas kernels  135 us (99%)
    pallas_call x1, Pallas kernels, on_device(): pl.pallas_call(functools.partial(kernel, dims, names), out_shape=(jax.Sha...  134 us

profile of v7, /device:TPU:1, one launch (start us, length us, event | category | flops | bytes accessed | tf_op | source)
XLA Modules:
  0.0 135.9 jit_solution(10104448738382738427)
XLA Ops:
  0.6 133.6 %shard_map.102 = (bf16[128,288]{1,0:T(8,128)(2,1)}, bf16[128,288]{1,0:T(8,128)(2,1)}, f32[18,288]{1,0:T(8,128)}, f32[18,288]{1,0:T(8,128)}) custom-call(bf16[128,288]{1,0:T(8,128)(2,1)} %bitcast.5, bf16[128,288]{1,0:T(8,128)(2,1)} %bitcast.6, f32[6,1,1152]{2,1,0:T(1,128)} %bitcast.7, bf16[18,3,288]{2,1,0:T(4,128)(2,1)} %qkv_s.1, bf16[18,288]{1,0:T(8,128)(2,1)} %out_s.1, ...), custom_call_target="tpu_custom_call" | custom-call | tf_op jit(solution)/shard_map/pallas_call | solution.py:723
  134.2 1.7 %shard_map.103 = (bf16[128,288]{1,0:T(8,128)(2,1)}, bf16[128,288]{1,0:T(8,128)(2,1)}, f32[18,288]{1,0:T(8,128)}, f32[18,288]{1,0:T(8,128)}) custom-call(bf16[128,288]{1,0:T(8,128)(2,1)} %get-tuple-element.12.refs_0_, bf16[128,288]{1,0:T(8,128)(2,1)} %get-tuple-element.13.refs_1_, f32[18,288]{1,0:T(8,128)} %get-tuple-element.14.refs_2_, ...), custom_call_target="tpu_custom_call" | custom-call | tf_op jit(solution)/shard_map/pallas_call | solution.py:738

commit v8 on v7

--- a/solution.py
+++ b/solution.py
@@ -607,13 +607,12 @@
     rsg_b[y] = rsg_a[y]
 
     out_partial(1, flat_t, rsp_a)
-    ex_send(lambda p: rsp_a.at[p], rsp_b, names["rsp"], Y, y, dev_y)
-    rsp_b[y] = rsp_a[y]
-
     ex_wait(rsg_b, names["rsg"], Y, y)
     z_put(fg_a, in_finish(1, rsg_b, xw_t, cot_t))
     ex_send(lambda p: fg_a.at[p], fg_b, names["fg_z"], Z, z, dev_z)
     fg_b[z] = fg_a[z]
+    ex_send(lambda p: rsp_a.at[p], rsp_b, names["rsp"], Y, y, dev_y)
+    rsp_b[y] = rsp_a[y]
 
     narrow([gw_t[n] for n in range(Y)])
     wg_start(1, flat_t)
@@ -622,8 +621,6 @@
     x_put(fg_c, from_z(flatten(fg_b)))
     ex_send(lambda p: fg_c.at[p], fg_d, names["fg_x"], G, g, dev_g)
     fg_d[g] = fg_c[g]
-    wg_second(1)
-
     ex_wait(rsp_b, names["rsp"], Y, y)
     second = xw_t[y].astype(F32) + mod[5, y] * add_up(rsp_b)
     z_put(out_a, second.astype(BF))
@@ -634,6 +631,7 @@
     fg_e[...] = from_groups(flatten(fg_d))
     gw_s[y] = gated(0, fg_e[...])
     ex_send(lambda p: gw_s.at[y], gw_s, names["ggs"], Y, y, dev_y)
+    wg_second(1)
 
     ex_wait(out_b, names["out_z"], Z, z)
     x_put(out_c, from_z(flatten(out_b)))

time: 136 us -> 135 us (level)
  no operation moved by 1% of the time
where the time goes in v8:
time: 135 us
  Pallas kernels  134 us (99%)
    pallas_call x1, Pallas kernels, on_device(): pl.pallas_call(functools.partial(kernel, dims, names), out_shape=(jax.Sha...  133 us

profile of v8, /device:TPU:1, one launch (start us, length us, event | category | flops | bytes accessed | tf_op | source)
XLA Modules:
  0.0 135.0 jit_solution(14607126881181138329)
XLA Ops:
  0.6 132.7 %shard_map.102 = (bf16[128,288]{1,0:T(8,128)(2,1)}, bf16[128,288]{1,0:T(8,128)(2,1)}, f32[18,288]{1,0:T(8,128)}, f32[18,288]{1,0:T(8,128)}) custom-call(bf16[128,288]{1,0:T(8,128)(2,1)} %bitcast.5, bf16[128,288]{1,0:T(8,128)(2,1)} %bitcast.6, f32[6,1,1152]{2,1,0:T(1,128)} %bitcast.7, bf16[18,3,288]{2,1,0:T(4,128)(2,1)} %qkv_s.1, bf16[18,288]{1,0:T(8,128)(2,1)} %out_s.1, ...), custom_call_target="tpu_custom_call" | custom-call | tf_op jit(solution)/shard_map/pallas_call | solution.py:721
  133.3 1.7 %shard_map.103 = (bf16[128,288]{1,0:T(8,128)(2,1)}, bf16[128,288]{1,0:T(8,128)(2,1)}, f32[18,288]{1,0:T(8,128)}, f32[18,288]{1,0:T(8,128)}) custom-call(bf16[128,288]{1,0:T(8,128)(2,1)} %get-tuple-element.12.refs_0_, bf16[128,288]{1,0:T(8,128)(2,1)} %get-tuple-element.13.refs_1_, f32[18,288]{1,0:T(8,128)} %get-tuple-element.14.refs_2_, ...), custom_call_target="tpu_custom_call" | custom-call | tf_op jit(solution)/shard_map/pallas_call | solution.py:736
